TPU v7x, 128 devices: a whole 4x4x4 slice. The times are simulated.
128 devices in a mesh: lat: 16 (over z_lo, y, core), lon: 8 (over z_hi, x).
Axes of the slice: x: 4, y: 4, z: 4 (z_hi: 2, z_lo: 2; z = z_hi * 2 + z_lo), core: 2. Of those that a mesh axis runs over, the one named last changes fastest.
Arguments:
- obs_values: float32 [128, 128, 2, 8, 128], P(('lat', 'lon')), may hold values from -6 to 6
- obs_cells: int32 [128, 128, 128], P(('lat', 'lon')), may hold values from 0 to 32767
- obs_counts: int32 [128, 128], P(('lat', 'lon')), may hold values from 32 to 128, as said below
- filter_lengths: float32 [2, 3], replicated, may hold values from 1 to 16
- filter_weights: float32 [2, 3], replicated, may hold values from 0.25 to 1
- vertical_mix: float32 [2, 8, 8], replicated, may hold values from -2 to 2
Outputs:
- increment: float32 [2, 8, 1024, 4096], P(None, None, 'lat', 'lon')
Inputs may be any that keep to these rules, and one draw needn't show every extreme that they name: `obs_counts`: every sending device fills all 128 slots toward some tiles.
All inputs are finite; a program needn't handle non-finite values.
Results may differ from a plain program's by a relative error of at most 0.000078.
Values sent between devices are 32-bit elements; how exact they have to be, the bound alone decides.
A program may use at most 576 MiB of HBM per device.

v0:
```python
import jax
import jax.numpy as jnp
from jax import lax
from jax.sharding import PartitionSpec as P

CLAT = 64
CLON = 512
LEV = 8
VARS = 2
HALF = 31


def padded(cells, sides, width, closed):
    for axis, dim in sides:
        count = lax.axis_size(axis)
        ends = count if closed else count - 1
        head = lax.slice_in_dim(cells, 0, width, axis=dim)
        tail = lax.slice_in_dim(cells, cells.shape[dim] - width, cells.shape[dim], axis=dim)
        cells = jnp.concatenate(
            [
                lax.ppermute(tail, axis, [(i, (i + 1) % count) for i in range(ends)]),
                cells,
                lax.ppermute(head, axis, [((i + 1) % count, i) for i in range(ends)]),
            ],
            axis=dim,
        )
    return cells


def kernels(lengths, weights):
    offsets = (jnp.arange(2 * HALF + 1) - HALF).astype(jnp.float32)
    profile = jnp.exp(-0.5 * (offsets[None, None, :] / lengths[:, :, None]) ** 2)
    filter_taps = jnp.sum(weights[:, :, None] * profile, axis=1)
    filter_taps = filter_taps / jnp.sqrt(jnp.sum(filter_taps * filter_taps, axis=1, keepdims=True))
    return jnp.repeat(filter_taps, LEV, axis=0)


def convolve(values_grid, filter_taps, direction):
    if direction == 2:
        kernel_shape = filter_taps[:, None, None, :]
    else:
        kernel_shape = filter_taps[:, None, :, None]
    result = lax.conv_general_dilated(
        values_grid[None],
        kernel_shape,
        (1, 1),
        "VALID",
        dimension_numbers=("NCHW", "OIHW", "NCHW"),
        feature_group_count=values_grid.shape[0],
        precision=lax.Precision.HIGHEST,
    )
    return result[0]


def local(obs_values, obs_cells, obs_counts, filter_lengths, filter_weights, vertical_mix):
    channels = VARS * LEV
    got_values, got_cells, got_counts = (
        lax.all_to_all(obs_values, ("lat", "lon"), split_axis=1, concat_axis=0, tiled=True),
        lax.all_to_all(obs_cells, ("lat", "lon"), split_axis=1, concat_axis=0, tiled=True),
        lax.all_to_all(obs_counts, ("lat", "lon"), split_axis=1, concat_axis=0, tiled=True),
    )
    sources = got_values.shape[0]
    capacity = got_values.shape[-1]
    slot_live = (jnp.arange(capacity)[None, :] < got_counts).astype(jnp.float32)
    weighted = got_values.reshape(sources, channels, capacity) * slot_live[:, None, :]
    spread = weighted.transpose(1, 0, 2).reshape(channels, sources * capacity)
    flat_cells = got_cells.reshape(-1)
    rows_onehot = ((flat_cells // CLON)[:, None] == jnp.arange(CLAT)[None, :]).astype(jnp.float32)
    cols_onehot = ((flat_cells % CLON)[:, None] == jnp.arange(CLON)[None, :]).astype(jnp.float32)
    stacked = spread[:, :, None] * rows_onehot[None, :, :]
    gridded = jnp.einsum("cjr,jk->crk", stacked, cols_onehot, precision=lax.Precision.HIGHEST)
    filter_taps = kernels(filter_lengths, filter_weights)
    rimmed = padded(gridded, (("lon", 2),), HALF, True)
    along_lon = convolve(rimmed, filter_taps, 2)
    rimmed_lat = padded(along_lon, (("lat", 1),), HALF, False)
    along_lat = convolve(rimmed_lat, filter_taps, 1)
    along_lat = along_lat.reshape(VARS, LEV, CLAT, CLON)
    return jnp.einsum("vlm,vmab->vlab", vertical_mix, along_lat, precision=lax.Precision.HIGHEST)


def solution(mesh):
    in_specs = (
        P(("lat", "lon"), None, None, None, None),
        P(("lat", "lon"), None, None),
        P(("lat", "lon"), None),
        P(),
        P(),
        P(),
    )
    out_specs = P(None, None, "lat", "lon")
    return jax.shard_map(local, mesh=mesh, in_specs=in_specs, out_specs=out_specs, check_vma=False)
```

profile of v0, /device:TPU:32, one launch (start us, length us, event | category | flops | bytes accessed | tf_op | source)
XLA Modules:
  0.0 480.7 jit_solution(16271994929324454959)
XLA Ops:
  1.4 10.2 %all-to-all-start.1 = ((s32[1,128,1]{2,0,1:T(1,128)}), s32[1,128,1]{2,0,1:T(1,128)S(1)}, u32[]{:S(2)}, u32[]{:S(2)}) async-start(s32[1,128,1]{2,0,1:T(1,128)} %copy.55), calls=%async_computation.1 | async-start | bytes 131072 | tf_op jit(solution)/shard_map/all_to_all | solution.py:60
  13.5 7.2 %all-to-all-done.1 = s32[1,128,1]{2,0,1:T(1,128)S(1)} async-done(((s32[1,128,1]{2,0,1:T(1,128)}), s32[1,128,1]{2,0,1:T(1,128)S(1)}, u32[]{:S(2)}, u32[]{:S(2)}) %all-to-all-start.1) | async-done | bytes 544 | tf_op jit(solution)/shard_map/all_to_all | solution.py:60
  20.6 4.8 %all-to-all-start.2 = ((s32[1,128,128]{2,0,1:T(1,128)}), s32[1,128,128]{2,0,1:T(1,128)S(1)}, u32[]{:S(2)}, u32[]{:S(2)}) async-start(s32[1,128,128]{2,0,1:T(1,128)} %bitcast.72), calls=%async_computation.2 | async-start | bytes 131072 | tf_op jit(solution)/shard_map/all_to_all | solution.py:59
  25.5 2.4 reduce
  27.9 6.5 %all-to-all-done.2 = s32[1,128,128]{2,0,1:T(1,128)S(1)} async-done(((s32[1,128,128]{2,0,1:T(1,128)}), s32[1,128,128]{2,0,1:T(1,128)S(1)}, u32[]{:S(2)}, u32[]{:S(2)}) %all-to-all-start.2) | async-done | bytes 65568 | tf_op jit(solution)/shard_map/all_to_all | solution.py:59
  34.5 4.9 %all-to-all-start = ((f32[1,128,2,8,128]{4,3,2,0,1:T(8,128)}), f32[1,128,2,8,128]{4,3,2,0,1:T(8,128)S(1)}, u32[]{:S(2)}, u32[]{:S(2)}) async-start(f32[1,128,2,8,128]{4,3,2,0,1:T(8,128)} %bitcast.70), calls=%async_computation | async-start | bytes 2097152 | tf_op jit(solution)/shard_map/all_to_all | solution.py:58
  39.4 2.3 fusion.16
  41.7 15.4 %all-to-all-done = f32[1,128,2,8,128]{4,3,2,0,1:T(8,128)S(1)} async-done(((f32[1,128,2,8,128]{4,3,2,0,1:T(8,128)}), f32[1,128,2,8,128]{4,3,2,0,1:T(8,128)S(1)}, u32[]{:S(2)}, u32[]{:S(2)}) %all-to-all-start) | async-done | bytes 1048608 | tf_op jit(solution)/shard_map/all_to_all | solution.py:58
  59.3 21.2 %fusion.49 = f32[16,16384,64]{1,2,0:T(8,128)} fusion(f32[16384,64]{0,1:T(8,128)S(1)} %copy-done.1, f32[16,16384]{1,0:T(8,128)S(1)} %bitcast.67), kind=kLoop, calls=%fused_computation.1.clone.2 | loop fusion | flops 16777216 | bytes 72351744 | tf_op jit(solution)/shard_map/cjr,jk->crk/dot_general | solution.py:71
  80.5 60.9 %fusion = f32[16,64,512]{2,1,0:T(8,128)S(1)} fusion(s32[16384]{0:T(1024)S(1)} %get-tuple-element.9, f32[16,16384,64]{1,2,0:T(8,128)} %fusion.49), kind=kOutput, calls=%fused_computation | convolution fusion | flops 103087603712 | bytes 69271552 | tf_op jit(solution)/shard_map/cjr,jk->crk/dot_general | solution.py:71
  142.3 5.1 %collective-permute-start.1 = (f32[16,64,31]{2,1,0:T(8,128)S(1)}, f32[16,64,31]{2,1,0:T(8,128)}, u32[]{:S(2)}, u32[]{:S(2)}) collective-permute-start(f32[16,64,31]{2,1,0:T(8,128)S(1)} %get-tuple-element.8), channel_id=1, source_target_pairs={{1,0},{2,1},{3,2},{4,3},{5,4},{6,5},{7,6},{0,7},{9,8},{10,9},{11,1... | collective-permute-start | bytes 380936 | tf_op jit(solution)/shard_map/ppermute | solution.py:23
  148.0 10.1 %collective-permute-done = f32[16,64,31]{2,1,0:T(8,128)} collective-permute-done((f32[16,64,31]{2,1,0:T(8,128)S(1)}, f32[16,64,31]{2,1,0:T(8,128)}, u32[]{:S(2)}, u32[]{:S(2)}) %collective-permute-start) | collective-permute-done | bytes 127008 | tf_op jit(solution)/shard_map/ppermute | solution.py:21
  158.1 2.1 maximum_bitcast_fusion
  160.4 3.2 reshape.126
  163.6 11.1 %copy.59 = f32[16,64,1,8,72]{0,3,4,1,2:T(8,128)} copy(f32[16,64,1,8,72]{4,3,1,0,2:T(8,128)} %reshape.126) | data formatting | bytes 4718592 | tf_op jit(solution)/shard_map/conv_general_dilated | solution.py:43
  174.7 11.3 %slice.21 = f32[16,64,1,7,62]{0,3,4,1,2:T(8,128)} slice(f32[16,64,1,8,72]{0,3,4,1,2:T(8,128)} %copy.59), slice={[0:16], [0:64], [0:1], [1:8], [0:62]} | slice | bytes 3555328 | tf_op jit(solution)/shard_map/conv_general_dilated | solution.py:43
  186.0 23.5 %fusion.51 = f32[16,64,8,134]{0,2,3,1:T(8,128)} fusion(f32[16,64,1,7,62]{0,3,4,1,2:T(8,128)} %slice.21, f32[16,64,1,8,72]{0,3,4,1,2:T(8,128)} %copy.59), kind=kLoop, calls=%fused_computation.3.clone.clone.clone.clone.1 | loop fusion | flops 3293184 | bytes 8527872 | tf_op jit(solution)/shard_map/conv_general_dilated | solution.py:43
  209.5 83.2 %broadcast_select_fusion = f32[64,8,72,16]{3,1,2,0:T(8,128)} fusion(pred[8,72]{0,1:T(8,128)(4,1)S(1)} %copy-done.3, f32[16,1,1,63]{0,1,3,2:T(1,128)S(1)} %copy.62, f32[16,64,8,134]{0,2,3,1:T(8,128)} %fusion.51), kind=kOutput, calls=%fused_computation.15 | convolution fusion | flops 446496768 | bytes 6754816 | tf_op jit(solution)/shard_map/conv_general_dilated | solution.py:43
  292.8 12.1 %copy.63 = f32[64,8,72,16]{2,1,3,0:T(8,128)} copy(f32[64,8,72,16]{3,1,2,0:T(8,128)} %broadcast_select_fusion) | data formatting | bytes 4718592 | tf_op jit(solution)/shard_map/conv_general_dilated | solution.py:43
  304.8 5.0 %reshape.130 = f32[64,1,576,16]{2,3,0,1:T(8,128)} reshape(f32[64,8,72,16]{2,1,3,0:T(8,128)} %copy.63) | data formatting | bytes 4718592 | tf_op jit(solution)/shard_map/conv_general_dilated | solution.py:43
  309.9 1.8 slice_bitcast_fusion
  312.9 2.1 collective-permute-start.2
  315.0 5.8 %collective-permute-start.3 = (f32[16,31,512]{2,0,1:T(8,128)S(1)}, f32[16,31,512]{2,0,1:T(8,128)}, u32[]{:S(2)}, u32[]{:S(2)}) collective-permute-start(f32[16,31,512]{2,0,1:T(8,128)S(1)} %get-tuple-element.6), channel_id=1, source_target_pairs={{8,0},{16,8},{24,16},{32,24},{40,32},{48,40},{56,48},{64,56},{72,6... | collective-permute-start | bytes 3047432 | tf_op jit(solution)/shard_map/ppermute | solution.py:23
  320.9 10.4 %collective-permute-done.2 = f32[16,31,512]{2,0,1:T(8,128)} collective-permute-done((f32[16,31,512]{2,0,1:T(8,128)}, f32[16,31,512]{2,0,1:T(8,128)}, u32[]{:S(2)}, u32[]{:S(2)}) %collective-permute-start.2) | collective-permute-done | bytes 1015840 | tf_op jit(solution)/shard_map/ppermute | solution.py:21
  332.7 4.2 pad_maximum_fusion
  336.9 5.4 %copy.64 = f32[16,126,512]{1,2,0:T(8,128)} copy(f32[16,126,512]{2,0,1:T(8,128)} %pad_maximum_fusion) | data formatting | bytes 8257536 | tf_op jit(solution)/shard_map/concatenate | solution.py:19
  342.3 26.7 %copy.65 = f32[16,126,8,64]{0,2,3,1:T(8,128)} copy(f32[16,126,8,64]{1,3,2,0:T(8,128)} %bitcast.66) | data formatting | bytes 8257536 | tf_op jit(solution)/shard_map/conv_general_dilated | solution.py:43
  369.0 92.3 %fusion.35 = f32[64,8,64,16]{3,1,2,0:T(8,128)} fusion(f32[16,126,8,64]{0,2,3,1:T(8,128)} %copy.65, f32[16,1,63,1]{0,1,3,2:T(1,128)S(1)} %copy.66), kind=kOutput, calls=%fused_computation.52 | convolution fusion | flops 396361728 | bytes 6229952 | tf_op jit(solution)/shard_map/conv_general_dilated | solution.py:43
  461.3 11.4 %copy.67 = f32[64,8,64,16]{2,1,3,0:T(8,128)} copy(f32[64,8,64,16]{3,1,2,0:T(8,128)} %fusion.35) | data formatting | bytes 4194304 | tf_op jit(solution)/shard_map/conv_general_dilated | solution.py:43
  472.7 3.4 reshape.137
  476.2 2.0 fusion.19
  478.2 2.5 copy.70
  (29 shorter events, 10.0 us)
Async XLA Ops:
  0.0 476.2 %copy-start = (f32[2,8,8]{2,1,0:T(8,128)S(1)}, f32[2,8,8]{2,1,0:T(8,128)}, u32[]{:S(2)}) copy-start(f32[2,8,8]{2,1,0:T(8,128)} %param.11) | copy-start | bytes 1540
  1.4 19.2 %all-to-all-start.1 = ((s32[1,128,1]{2,0,1:T(1,128)}), s32[1,128,1]{2,0,1:T(1,128)S(1)}, u32[]{:S(2)}, u32[]{:S(2)}) async-start(s32[1,128,1]{2,0,1:T(1,128)} %copy.55), calls=%async_computation.1 | async-start | bytes 131072 | tf_op jit(solution)/shard_map/all_to_all | solution.py:60
  20.6 13.8 %all-to-all-start.2 = ((s32[1,128,128]{2,0,1:T(1,128)}), s32[1,128,128]{2,0,1:T(1,128)S(1)}, u32[]{:S(2)}, u32[]{:S(2)}) async-start(s32[1,128,128]{2,0,1:T(1,128)} %bitcast.72), calls=%async_computation.2 | async-start | bytes 131072 | tf_op jit(solution)/shard_map/all_to_all | solution.py:59
  34.5 22.6 %all-to-all-start = ((f32[1,128,2,8,128]{4,3,2,0,1:T(8,128)}), f32[1,128,2,8,128]{4,3,2,0,1:T(8,128)S(1)}, u32[]{:S(2)}, u32[]{:S(2)}) async-start(f32[1,128,2,8,128]{4,3,2,0,1:T(8,128)} %bitcast.70), calls=%async_computation | async-start | bytes 2097152 | tf_op jit(solution)/shard_map/all_to_all | solution.py:58
  57.1 2.2 copy-start.1
  141.6 16.5 %collective-permute-start = (f32[16,64,31]{2,1,0:T(8,128)S(1)}, f32[16,64,31]{2,1,0:T(8,128)}, u32[]{:S(2)}, u32[]{:S(2)}) collective-permute-start(f32[16,64,31]{2,1,0:T(8,128)S(1)} %get-tuple-element.7), channel_id=1, source_target_pairs={{0,1},{1,2},{2,3},{3,4},{4,5},{5,6},{6,7},{7,0},{8,9},{9,10},{10,1... | collective-permute-start | bytes 380936 | tf_op jit(solution)/shard_map/ppermute | solution.py:21
  142.3 15.9 %collective-permute-start.1 = (f32[16,64,31]{2,1,0:T(8,128)S(1)}, f32[16,64,31]{2,1,0:T(8,128)}, u32[]{:S(2)}, u32[]{:S(2)}) collective-permute-start(f32[16,64,31]{2,1,0:T(8,128)S(1)} %get-tuple-element.8), channel_id=1, source_target_pairs={{1,0},{2,1},{3,2},{4,3},{5,4},{6,5},{7,6},{0,7},{9,8},{10,9},{11,1... | collective-permute-start | bytes 380936 | tf_op jit(solution)/shard_map/ppermute | solution.py:23
  186.0 23.5 %copy-start.3 = (pred[8,72]{0,1:T(8,128)(4,1)S(1)}, pred[8,72]{0,1:T(8,128)(4,1)}, u32[]{:S(2)}) copy-start(pred[8,72]{0,1:T(8,128)(4,1)} %constant.50) | copy-start | bytes 1732
  309.9 10.9 %copy-start.2 = (f32[16,1,63,1]{2,0,3,1:T(8,128)S(1)}, f32[16,1,63,1]{2,0,3,1:T(8,128)}, u32[]{:S(2)}) copy-start(f32[16,1,63,1]{2,0,3,1:T(8,128)} %get-tuple-element.11) | copy-start | bytes 12100
  312.9 18.4 %collective-permute-start.2 = (f32[16,31,512]{2,0,1:T(8,128)}, f32[16,31,512]{2,0,1:T(8,128)}, u32[]{:S(2)}, u32[]{:S(2)}) collective-permute-start(f32[16,31,512]{2,0,1:T(8,128)} %get-tuple-element.5), channel_id=1, source_target_pairs={{0,8},{8,16},{16,24},{24,32},{32,40},{40,48},{48,56},{56,64},{64,7... | collective-permute-start | bytes 3047432 | tf_op jit(solution)/shard_map/ppermute | solution.py:21
  315.0 17.7 %collective-permute-start.3 = (f32[16,31,512]{2,0,1:T(8,128)S(1)}, f32[16,31,512]{2,0,1:T(8,128)}, u32[]{:S(2)}, u32[]{:S(2)}) collective-permute-start(f32[16,31,512]{2,0,1:T(8,128)S(1)} %get-tuple-element.6), channel_id=1, source_target_pairs={{8,0},{16,8},{24,16},{32,24},{40,32},{48,40},{56,48},{64,56},{72,6... | collective-permute-start | bytes 3047432 | tf_op jit(solution)/shard_map/ppermute | solution.py:23
where the time goes:
time: 486 us; the launch traced here: 481 us
  matrix products  238 us (49%)
  local copies, waits for them, and re-layouts  101 us (21%)
  other arithmetic  56.5 us (12%)
  waiting for transfers between devices  51 us (10%)
  starting transfers between devices  33.5 us (7%)
    conv_general_dilated x2, matrix products, convolve(): lax.conv_general_dilated(values_grid[None], kernel_shape, (1, 1), 'VALID'...  176 us
    conv_general_dilated x8, local copies, waits for them, and re-layouts, convolve(): lax.conv_general_dilated(values_grid[None], kernel_shape, (1, 1), 'VALID'...  84.2 us
    dot_general x1, matrix products, local(): jnp.einsum('cjr,jk->crk', stacked, cols_onehot, precision=lax.Precision.H...  60.9 us
    conv_general_dilated x1, other arithmetic, convolve(): lax.conv_general_dilated(values_grid[None], kernel_shape, (1, 1), 'VALID'...  23.5 us
    dot_general x1, other arithmetic, local(): jnp.einsum('cjr,jk->crk', stacked, cols_onehot, precision=lax.Precision.H...  21.2 us
    ppermute x2, waiting for transfers between devices, padded(): lax.ppermute(tail, axis, [(i, (i + 1) % count) for i in range(ends)])  20.5 us
    all_to_all x1, waiting for transfers between devices, local(): lax.all_to_all(obs_values, ('lat', 'lon'), split_axis=1, concat_axis=0, t...  15.4 us
    ppermute x2, starting transfers between devices, padded(): lax.ppermute(head, axis, [((i + 1) % count, i) for i in range(ends)])  10.8 us
  transfers between devices with their start and end apart: 7, of which 6 were waited for; matrix products, arithmetic and copies ran while one was open for 2% of the time, Pallas kernels for 0%

commit v1 on v0

v1 whole, which is shorter than its diff:
```python
import functools

import jax
import jax.numpy as jnp
import numpy as np
from jax import lax
from jax.experimental import pallas as pl
from jax.experimental.pallas import tpu as pltpu
from jax.sharding import PartitionSpec as P

HALF = 31
LEV = 8
BITREV = (0, 4, 2, 6, 1, 5, 3, 7)
NACC = 2
MESH = pl.DeviceIdType.MESH


def split(x):
    hi = x.astype(jnp.bfloat16)
    return hi, (x - hi.astype(jnp.float32)).astype(jnp.bfloat16)


def dot(a, b):
    return jnp.dot(a, b, preferred_element_type=jnp.float32)


def dot3(a, b):
    return dot(a[0], b[0]) + dot(a[1], b[0]) + dot(a[0], b[1])


def grid_kernel(vals_hbm, cells_hbm, mixer, out, edges, vals, cells_v, cells_t, cells, table, sems, *grids):
    copies = [
        pltpu.make_async_copy(vals_hbm.at[pl.ds(q * 32, 32)], vals.at[pl.ds(q * 32, 32)], sems.at[q])
        for q in range(4)
    ]
    cell_copy = pltpu.make_async_copy(cells_hbm, cells_v, sems.at[4])
    cell_copy.start()
    for copy in copies:
        copy.start()
    cell_copy.wait()
    cells_t[...] = cells_v[...].T
    to_smem = pltpu.make_async_copy(cells_t, cells, sems.at[5])
    to_smem.start()

    def clear(i, carry):
        for grid in grids:
            grid[pl.ds(pl.multiple_of(i * 256, 256), 256), :] = jnp.zeros((256, 128), jnp.float32)
        return carry

    lax.fori_loop(0, 32768 // 256, clear, 0)
    mix = split(mixer[...])
    for copy in copies:
        copy.wait()

    def mix_rows(step, carry):
        for u in range(4):
            sg = step * 4 + u
            v = vals[pl.ds(pl.multiple_of(sg * 8, 8), 8)].reshape(128, 128).T
            table[pl.ds(pl.multiple_of(sg * 128, 128), 128), :] = dot3(split(v), mix)
        return carry

    lax.fori_loop(0, 4, mix_rows, 0)
    lane = lax.broadcasted_iota(jnp.int32, (1, 128), 1) // 16
    masks = [lane == i for i in range(8)]
    to_smem.wait()

    def scatter(j, carry):
        for g0 in range(0, 16, NACC):
            updates = []
            for a in range(NACC):
                sg = g0 + a
                row = table[pl.ds(sg * 128 + j, 1), :]
                for i in range(8):
                    c = cells[j, sg * 8 + i]
                    updates.append((a, i, c, grids[a][pl.ds(c, 1), :] + row))
            for a, i, c, total in updates:
                pltpu.store(grids[a].at[pl.ds(c, 1), :], total, mask=masks[i])
        return carry

    lax.fori_loop(0, 128, scatter, 0)

    lane8 = lax.broadcasted_iota(jnp.int32, (8, 128), 1) // 16
    b0 = (lane8 & 1) == 0
    b1 = (lane8 & 2) == 0
    b2 = (lane8 & 4) == 0
    packed = table

    def gather(t, carry):
        for u in range(2):
            base = t * 16 + u * 8
            a = []
            for q in range(8):
                off = pl.multiple_of(BITREV[q] * 4096 + base, 8)
                x = grids[0][pl.ds(off, 8), :]
                for grid in grids[1:]:
                    x = x + grid[pl.ds(off, 8), :]
                a.append(x)
            b = [
                jnp.where(b0, a[q], a[q + 4]) + pltpu.roll(jnp.where(b0, a[q + 4], a[q]), 16, 1)
                for q in range(4)
            ]
            c = [
                jnp.where(b1, b[q], b[q + 2]) + pltpu.roll(jnp.where(b1, b[q + 2], b[q]), 32, 1)
                for q in range(2)
            ]
            d = jnp.where(b2, c[0], c[1]) + pltpu.roll(jnp.where(b2, c[1], c[0]), 64, 1)
            packed[pl.ds(pl.multiple_of(base, 8), 8), :] = d
        return carry

    lax.fori_loop(0, 256, gather, 0)

    def turn(k2, carry):
        for cb in range(4):
            block = packed[pl.ds(pl.multiple_of(k2 * 512 + cb * 128, 128), 128), :].T
            block = block.reshape(8, 2, 8, 128)
            for v in range(2):
                for h in range(2):
                    out[h, v, k2, :, :, pl.ds(cb * 128, 128)] = block[h * 4 : h * 4 + 4, v]
        return carry

    lax.fori_loop(0, 8, turn, 0)

    quarter = lax.broadcasted_iota(jnp.int32, (32, 128), 1) // 32
    for h in range(2):
        for v in range(2):
            for kk in range(2):
                for side, (col, at) in enumerate(((0, 0), (384, 96))):
                    total = None
                    for kq in range(4):
                        x = out[h, v, kk * 4 + kq, :, :, pl.ds(col, 128)].reshape(32, 128)
                        shift = (kq * 32 - at) % 128
                        x = pltpu.roll(x, shift, 1) if shift else x
                        total = x if total is None else jnp.where(quarter == kq, x, total)
                    edges[side, h, v, pl.ds(kk * 32, 32), :] = total


def grid_tile(vals, cells, mixer):
    return pl.pallas_call(
        grid_kernel,
        out_shape=(
            jax.ShapeDtypeStruct((2, 2, 8, 4, 8, 512), jnp.float32),
            jax.ShapeDtypeStruct((2, 2, 2, 64, 128), jnp.float32),
        ),
        in_specs=[
            pl.BlockSpec(memory_space=pl.ANY),
            pl.BlockSpec(memory_space=pl.ANY),
            pl.BlockSpec(memory_space=pltpu.VMEM),
        ],
        out_specs=[pl.BlockSpec(memory_space=pltpu.VMEM)] * 2,
        scratch_shapes=[
            pltpu.VMEM((128, 16, 128), jnp.float32),
            pltpu.VMEM((128, 128), jnp.int32),
            pltpu.VMEM((128, 128), jnp.int32),
            pltpu.SMEM((128, 128), jnp.int32),
            pltpu.VMEM((4096, 128), jnp.float32),
            pltpu.SemaphoreType.DMA((6,)),
        ]
        + [pltpu.VMEM((32768, 128), jnp.float32)] * NACC,
        compiler_params=pltpu.CompilerParams(vmem_limit_bytes=60 * 2**20),
        cost_estimate=pl.CostEstimate(flops=10**9, bytes_accessed=4 * 2**20, transcendentals=0),
        name="scatter",
    )(vals, cells, mixer)


ROWS = np.concatenate([[base + rg * 8 + k2 for k2 in range(8) for rg in range(4)] for base in (0, 32, -32, 64)])


def filter_kernel(n_lat, n_lon, x_hbm, e_hbm, thi, tlo, whi, wlo, ahi, alo, out, x, e, y, send, recv, local):
    lat = lax.axis_index("lat")
    lon = lax.axis_index("lon")
    west = lax.rem(lon + n_lon - 1, n_lon)
    east = lax.rem(lon + 1, n_lon)
    north = lat - 1
    south = lat + 1
    has_north = lat > 0
    has_south = lat < n_lat - 1

    own_x = pltpu.make_async_copy(x_hbm, x.at[pl.ds(0, 2)], local.at[0])
    own_x.start()

    barrier = pltpu.get_barrier_semaphore()

    def greet(where):
        pl.semaphore_signal(barrier, inc=1, device_id=where, device_id_type=MESH)

    greet((lat, west))
    greet((lat, east))

    @pl.when(has_north)
    def _():
        for side in (west, lon, east):
            greet((north, side))

    @pl.when(has_south)
    def _():
        for side in (west, lon, east):
            greet((south, side))

    ends = lat * (n_lat - 1 - lat)
    pl.semaphore_wait(barrier, jnp.where(ends == 0, 5, 8))

    def remote(src, dst, slot, where):
        return pltpu.make_async_remote_copy(
            src_ref=src, dst_ref=dst, send_sem=send.at[slot], recv_sem=recv.at[slot],
            device_id=where, device_id_type=MESH,
        )

    sides = [
        remote(e_hbm.at[0], e.at[1, pl.ds(0, 2)], 0, (lat, west)),
        remote(e_hbm.at[1], e.at[0, pl.ds(0, 2)], 1, (lat, east)),
    ]
    up = [
        remote(e_hbm.at[0, 0], e.at[1, 3], 2, (north, west)),
        remote(e_hbm.at[1, 0], e.at[0, 3], 3, (north, east)),
        remote(x_hbm.at[0, 0], x.at[3, 0], 4, (north, lon)),
        remote(x_hbm.at[0, 1], x.at[3, 1], 5, (north, lon)),
    ]
    down = [
        remote(e_hbm.at[0, 1], e.at[1, 2], 6, (south, west)),
        remote(e_hbm.at[1, 1], e.at[0, 2], 7, (south, east)),
        remote(x_hbm.at[1, 0], x.at[2, 0], 8, (south, lon)),
        remote(x_hbm.at[1, 1], x.at[2, 1], 9, (south, lon)),
    ]
    for copy in sides:
        copy.start()

    @pl.when(has_north)
    def _():
        for copy in up:
            copy.start()

    @pl.when(has_south)
    def _():
        for copy in down:
            copy.start()

    @pl.when(jnp.logical_not(has_north))
    def _():
        x[2] = jnp.zeros((2, 256, 512), jnp.float32)
        e[:, 2] = jnp.zeros((2, 2, 64, 128), jnp.float32)

    @pl.when(jnp.logical_not(has_south))
    def _():
        x[3] = jnp.zeros((2, 256, 512), jnp.float32)
        e[:, 3] = jnp.zeros((2, 2, 64, 128), jnp.float32)

    def along_lon(s, v):
        rows = dot3(split(x[s, v]), (thi[v], tlo[v]))
        for cb in range(4):
            y[s, v, cb] = rows[:, cb * 128 : cb * 128 + 128]
        for side in range(2):
            rim = dot3(split(e[side, s, v]), (whi[v, side], wlo[v, side]))
            for kk in range(2):
                for kq in range(4):
                    at = pl.ds((kk * 4 + kq) * 32, 32)
                    y[s, v, side * 3, at] += rim[kk * 32 : kk * 32 + 32, kq * 128 : kq * 128 + 128]

    def along_lat(v):
        a = ahi[v], alo[v]

        def level(l, carry):
            rows = jnp.concatenate(
                [
                    jnp.concatenate([y[s, v, cb, pl.ds(l, 32, stride=8), :] for cb in range(4)], axis=1)
                    for s in range(4)
                ],
                axis=0,
            )
            out[v, l] = dot3(a, split(rows))
            return carry

        lax.fori_loop(0, LEV, level, 0)

    own_x.wait()
    for copy in sides:
        copy.wait_recv()

    def own(i, carry):
        along_lon(i // 2, i % 2)
        return carry

    lax.fori_loop(0, 4, own, 0)

    for v in range(2):
        @pl.when(has_north)
        def _():
            if v == 0:
                down[0].wait_recv()
                down[1].wait_recv()
            down[2 + v].wait_recv()

        @pl.when(has_south)
        def _():
            if v == 0:
                up[0].wait_recv()
                up[1].wait_recv()
            up[2 + v].wait_recv()

        lax.fori_loop(2, 4, lambda s, carry: (along_lon(s, v), carry)[1], 0)
        along_lat(v)

    for copy in sides:
        copy.wait_send()

    @pl.when(has_north)
    def _():
        for copy in up:
            copy.wait_send()

    @pl.when(has_south)
    def _():
        for copy in down:
            copy.wait_send()


def filter_tile(n_lat, n_lon, x, e, weights):
    return pl.pallas_call(
        functools.partial(filter_kernel, n_lat, n_lon),
        out_shape=jax.ShapeDtypeStruct((2, 8, 64, 512), jnp.float32),
        in_specs=[pl.BlockSpec(memory_space=pl.ANY)] * 2 + [pl.BlockSpec(memory_space=pltpu.VMEM)] * 6,
        out_specs=pl.BlockSpec(memory_space=pltpu.VMEM),
        scratch_shapes=[
            pltpu.VMEM((4, 2, 256, 512), jnp.float32),
            pltpu.VMEM((2, 4, 2, 64, 128), jnp.float32),
            pltpu.VMEM((4, 2, 4, 256, 128), jnp.float32),
            pltpu.SemaphoreType.DMA((10,)),
            pltpu.SemaphoreType.DMA((10,)),
            pltpu.SemaphoreType.DMA((1,)),
        ],
        compiler_params=pltpu.CompilerParams(
            vmem_limit_bytes=48 * 2**20, collective_id=0, has_side_effects=True
        ),
        cost_estimate=pl.CostEstimate(flops=6 * 10**9, bytes_accessed=8 * 2**20, transcendentals=0),
        name="filters",
    )(x, e, *weights)


def band_weights(lengths, weights):
    def profile(offset):
        t = offset.astype(np.float32)
        shape = (2,) + (1,) * t.ndim
        total = 0.0
        for s in range(lengths.shape[1]):
            scale = t[None] / lengths[:, s].reshape(shape)
            total = total + weights[:, s].reshape(shape) * jnp.exp(-0.5 * scale**2)
        return jnp.where(np.abs(offset)[None] <= HALF, total, 0.0)

    taps = profile(np.arange(-HALF, HALF + 1))
    norm = lax.rsqrt(jnp.sum(taps * taps, axis=1))

    def band(offset):
        x = profile(offset) * norm.reshape((2,) + (1,) * offset.ndim)
        hi = lax.reduce_precision(x, 8, 7)
        return hi.astype(jnp.bfloat16), (x - hi).astype(jnp.bfloat16)

    c = np.arange(512)
    centre = band(c[:, None] - c[None, :])
    lane = np.arange(128)
    kq, t = lane // 32, lane % 32
    same = kq[:, None, None] == np.arange(4)[None, :, None]
    col = np.arange(128)[None, None, :]
    far = 10 * HALF
    left = np.where(same, (t - 32)[:, None, None] - col, far)
    right = np.where(same, (t + 128)[:, None, None] - col, far)
    rims = band(np.stack([left, right]).reshape(2, 128, 512))
    down = band(ROWS[None, :] - np.arange(64)[:, None])
    return centre + rims + down


def local(obs_values, obs_cells, obs_counts, filter_lengths, filter_weights, vertical_mix):
    live = jnp.arange(128)[None, :] < obs_counts[0][:, None]
    vals = jnp.where(live[:, None, :], obs_values[0].reshape(128, 16, 128), 0.0)
    axes = ("lat", "lon")
    cells = lax.all_to_all(obs_cells[0], axes, split_axis=0, concat_axis=0, tiled=True)
    vals = lax.all_to_all(vals, axes, split_axis=0, concat_axis=0, tiled=True)
    eye = jnp.eye(8, dtype=jnp.float32)
    both = jnp.einsum("vlm,vw->vmwl", vertical_mix, jnp.eye(2, dtype=jnp.float32), precision=lax.Precision.HIGHEST)
    mixer = (eye[:, None, :, None] * both.reshape(16, 16)[None, :, None, :]).reshape(128, 128)
    weights = band_weights(filter_lengths, filter_weights)
    x, e = grid_tile(vals, cells, mixer)
    return filter_tile(lax.axis_size("lat"), lax.axis_size("lon"), x.reshape(2, 2, 256, 512), e, weights)


def solution(mesh):
    in_specs = (
        P(("lat", "lon"), None, None, None, None),
        P(("lat", "lon"), None, None),
        P(("lat", "lon"), None),
        P(),
        P(),
        P(),
    )
    return jax.shard_map(
        local, mesh=mesh, in_specs=in_specs, out_specs=P(None, None, "lat", "lon"), check_vma=False
    )
```

time: 486 us -> 153 us (0.31); the launches traced: 481 us -> 153 us
  matrix products: 238 us -> 0 us
  Pallas kernels: 0 us -> 105 us
  local copies, waits for them, and re-layouts: 101 us -> 6.07 us
  other arithmetic: 56.5 us -> 8.23 us
  waiting for transfers between devices: 51 us -> 14.2 us
  starting transfers between devices: 33.5 us -> 19.5 us
    conv_general_dilated x2 -> x0, matrix products: 176 us -> none  [convolve(): lax.conv_general_dilated(values_grid[None], kernel_shape, (1, 1), 'VALID'...]
    pallas_call x0 -> x2, Pallas kernels: none -> 105 us  [the longest x1 78.4 us: grid_tile(): pl.pallas_call(grid_kernel, out_shape=(jax.ShapeDtypeStruct((2, 2, 8, 4,...]
    conv_general_dilated x8 -> x0, local copies, waits for them, and re-layouts: 84.2 us -> none  [convolve(): lax.conv_general_dilated(values_grid[None], kernel_shape, (1, 1), 'VALID'...]
    dot_general x2 -> x0, matrix products: 62.9 us -> none  [the longest x1 60.9 us: local(): jnp.einsum('cjr,jk->crk', stacked, cols_onehot, precision=lax.Precision.H...]
    conv_general_dilated x1 -> x0, other arithmetic: 23.5 us -> none  [convolve(): lax.conv_general_dilated(values_grid[None], kernel_shape, (1, 1), 'VALID'...]
    ppermute x4 -> x0, waiting for transfers between devices: 21.9 us -> none  [the longest x2 20.5 us: padded(): lax.ppermute(tail, axis, [(i, (i + 1) % count) for i in range(ends)])]
    dot_general x1 -> x0, other arithmetic: 21.2 us -> none  [local(): jnp.einsum('cjr,jk->crk', stacked, cols_onehot, precision=lax.Precision.H...]
    all_to_all x3 -> x2, waiting for transfers between devices: 29.1 us -> 14.2 us  [the longest x1 13.2 us: local(): vals = lax.all_to_all(vals, axes, split_axis=0, concat_axis=0, tiled=True)]
  transfers between devices with their start and end apart: 7 -> 2, of which waited for: 6 -> 2; matrix products, arithmetic and copies ran while one was open for 2% -> 8% of each run, Pallas kernels for 0% -> 0%
where the time goes in v1:
time: 153 us
  Pallas kernels  105 us (69%)
  starting transfers between devices  19.5 us (13%)
  waiting for transfers between devices  14.2 us (9%)
  other arithmetic  8.23 us (5%)
  local copies, waits for them, and re-layouts  6.07 us (4%)
    pallas_call x1, Pallas kernels, grid_tile(): pl.pallas_call(grid_kernel, out_shape=(jax.ShapeDtypeStruct((2, 2, 8, 4,...  78.4 us
    pallas_call x1, Pallas kernels, filter_tile(): pl.pallas_call(functools.partial(filter_kernel, n_lat, n_lon), out_shape=...  26.2 us
    all_to_all x1, waiting for transfers between devices, local(): vals = lax.all_to_all(vals, axes, split_axis=0, concat_axis=0, tiled=True)  13.2 us
    all_to_all x1, starting transfers between devices, local(): lax.all_to_all(obs_cells[0], axes, split_axis=0, concat_axis=0, tiled=True)  10.2 us
    all_to_all x1, starting transfers between devices, local(): vals = lax.all_to_all(vals, axes, split_axis=0, concat_axis=0, tiled=True)  9.27 us
    unnamed x22, local copies, waits for them, and re-layouts  4.13 us
    convert_element_type x3, other arithmetic, band(): return (hi.astype(jnp.bfloat16), (x - hi).astype(jnp.bfloat16))  4.12 us
  transfers between devices with their start and end apart: 2, of which 2 were waited for; matrix products, arithmetic and copies ran while one was open for 8% of the time, Pallas kernels for 0%

profile of v1, /device:TPU:32, one launch (start us, length us, event | category | flops | bytes accessed | tf_op | source)
XLA Modules:
  0.0 152.8 jit_solution(9277386990080530003)
XLA Ops:
  0.0 10.2 %all-to-all-start.1 = ((s32[128,1,128]{2,1,0:T(1,128)}), s32[128,1,128]{2,1,0:T(1,128)S(1)}, u32[]{:S(2)}, u32[]{:S(2)}) async-start(s32[128,1,128]{2,1,0:T(1,128)} %bitcast.11), calls=%async_computation.1 | async-start | bytes 131072 | tf_op jit(solution)/shard_map/all_to_all | solution.py:374
  10.3 1.0 slice_reduce_fusion.4
  11.3 0.0 copy-start.6
  11.3 0.9 fusion.55
  12.2 0.0 copy-start.8
  12.2 0.8 copy.25
  13.0 0.1 multiply_bitcast_fusion
  13.0 0.1 mul.185
  13.1 0.7 iota_compare_fusion
  13.9 1.0 copy.28
  14.8 2.3 %bitcast_select_fusion = f32[128,16,128]{2,1,0:T(8,128)} fusion(f32[1,128,2,8,128]{4,3,2,1,0:T(8,128)} %param.22, pred[128,128]{1,0:T(8,128)(4,1)S(1)} %iota_compare_fusion), kind=kLoop, calls=%fused_computation.38 | loop fusion | flops 262144 | bytes 2113536 | tf_op jit(solution)/shard_map/jit(_where)/select_n | solution.py:372
  17.2 0.0 copy-done.1
  17.2 1.0 fusion.27
  18.1 0.1 broadcast_multiply_fusion
  18.3 1.0 all-to-all-done.1
  19.2 9.3 %all-to-all-start = ((f32[128,16,128]{2,1,0:T(8,128)}), f32[128,16,128]{2,1,0:T(8,128)}, u32[]{:S(2)}, u32[]{:S(2)}) async-start(f32[128,16,128]{2,1,0:T(8,128)} %bitcast_select_fusion), calls=%async_computation | async-start | bytes 2097152 | tf_op jit(solution)/shard_map/all_to_all | solution.py:375
  28.5 0.0 copy-done.8
  28.5 0.0 copy-done.4
  28.5 0.0 copy-done.7
  28.5 0.1 fusion.41
  28.7 0.0 copy-done.2
  28.7 0.1 copy.27
  28.8 0.0 copy-done.5
  28.8 0.0 copy-done.6
  28.8 0.8 mul.188.mixer
  29.6 3.0 %fusion.13 = (bf16[2,512,512]{2,1,0:T(8,128)(2,1)S(1)}, bf16[2,512,512]{2,1,0:T(8,128)(2,1)S(1)}) fusion(f32[2]{0:T(128)} %copy-done.8, f32[2]{0:T(128)S(1)} %get-tuple-element.10, f32[2]{0:T(128)} %copy-done.5, f32[2]{0:T(128)S(1)} %get-tuple-element.11, f32[2]{0:T(128)S(1)} %get-tuple-element.21, f32[2]{0:T(128)S(1)} %get-tuple-element.9, ...), kind=kLoop, calls=%fused_computation.18 | loop fusion | flops 10485760 | bytes 3407928 | tf_op jit(solution)/shard_map/convert_element_type | solution.py:354
  32.7 0.0 copy-done.3
  32.7 13.2 %all-to-all-done.vals_hbm = f32[128,16,128]{2,1,0:T(8,128)} async-done(((f32[128,16,128]{2,1,0:T(8,128)}), f32[128,16,128]{2,1,0:T(8,128)}, u32[]{:S(2)}, u32[]{:S(2)}) %all-to-all-start) | async-done | bytes 1048608 | tf_op jit(solution)/shard_map/all_to_all | solution.py:375
  45.9 78.4 %scatter.1 = (f32[2,2,8,4,8,512]{5,4,3,2,1,0:T(8,128)}, f32[2,2,2,64,128]{4,3,2,1,0:T(8,128)}) custom-call(f32[128,16,128]{2,1,0:T(8,128)} %all-to-all-done.vals_hbm, s32[128,128]{1,0:T(8,128)} %bitcast.12, f32[128,128]{1,0:T(8,128)} %mul.188.mixer), custom_call_target="tpu_custom_call" | custom-call | flops 1000000000 | bytes 4194304 | tf_op jit(solution)/shard_map/scatter/pallas_call | solution.py:138
  124.3 0.9 copy-done
  125.2 26.2 %filters.1 = f32[2,8,64,512]{3,2,1,0:T(8,128)S(1)} custom-call(f32[2,2,256,512]{3,2,1,0:T(8,128)} %bitcast.15, f32[2,2,2,64,128]{4,3,2,1,0:T(8,128)S(1)} %copy-done, bf16[2,512,512]{2,1,0:T(8,128)(2,1)S(1)} %get-tuple-element.16.thi, bf16[2,512,512]{2,1,0:T(8,128)(2,1)S(1)} %get-tuple-element.15.tlo, bf16[2,2,128,512]{3,2,1,0:T(8,128)(2,1)S(1)} %get-tuple-element.18.whi, ...), custom_call_target="tpu_custom_call" | custom-call | flops 6000000000 | bytes 8388608 | tf_op jit(solution)/shard_map/filters/pallas_call | solution.py:317
  151.5 1.3 copy.29
  (10 shorter events, 0.0 us)
Async XLA Ops:
  0.0 17.2 %copy-start.1 = (f32[2,128,512]{2,1,0:T(8,128)S(1)}, f32[2,128,512]{2,1,0:T(8,128)}, u32[]{:S(2)}) copy-start(f32[2,128,512]{2,1,0:T(8,128)} %constant.38) | copy-start | bytes 1572868
  0.0 19.2 %all-to-all-start.1 = ((s32[128,1,128]{2,1,0:T(1,128)}), s32[128,1,128]{2,1,0:T(1,128)S(1)}, u32[]{:S(2)}, u32[]{:S(2)}) async-start(s32[128,1,128]{2,1,0:T(1,128)} %bitcast.11), calls=%async_computation.1 | async-start | bytes 131072 | tf_op jit(solution)/shard_map/all_to_all | solution.py:374
  11.3 17.5 %copy-start.5 = (f32[2]{0:T(128)}, f32[2]{0:T(128)S(1)}, u32[]{:S(2)}) copy-start(f32[2]{0:T(128)S(1)} %get-tuple-element.22) | copy-start | bytes 28
  11.3 17.5 %copy-start.6 = (f32[2]{0:T(128)}, f32[2]{0:T(128)S(1)}, u32[]{:S(2)}) copy-start(f32[2]{0:T(128)S(1)} %get-tuple-element.23) | copy-start | bytes 28
  12.2 16.3 %copy-start.8 = (f32[2]{0:T(128)}, f32[2]{0:T(128)S(1)}, u32[]{:S(2)}) copy-start(f32[2]{0:T(128)S(1)} %rsqrt.11) | copy-start | bytes 28
  17.2 11.4 %copy-start.4 = (f32[64,128]{1,0:T(8,128)S(1)}, f32[64,128]{1,0:T(8,128)}, u32[]{:S(2)}) copy-start(f32[64,128]{1,0:T(8,128)} %constant.40) | copy-start | bytes 98308
  17.2 11.4 %copy-start.7 = (pred[64,128]{1,0:T(32,128)(4,1)S(1)}, pred[64,128]{1,0:T(32,128)(4,1)}, u32[]{:S(2)}) copy-start(pred[64,128]{1,0:T(32,128)(4,1)} %constant.39) | copy-start | bytes 24580
  17.2 11.5 %copy-start.2 = (pred[512,512]{1,0:T(32,128)(4,1)S(1)}, pred[512,512]{1,0:T(32,128)(4,1)}, u32[]{:S(2)}) copy-start(pred[512,512]{1,0:T(32,128)(4,1)} %constant.34) | copy-start | bytes 786436
  19.2 13.4 %copy-start.3 = (s32[128,1,128]{2,1,0:T(1,128)}, s32[128,1,128]{2,1,0:T(1,128)S(1)}, u32[]{:S(2)}) copy-start(s32[128,1,128]{2,1,0:T(1,128)S(1)} %all-to-all-done.1) | copy-start | bytes 196612
  19.2 26.7 %all-to-all-start = ((f32[128,16,128]{2,1,0:T(8,128)}), f32[128,16,128]{2,1,0:T(8,128)}, u32[]{:S(2)}, u32[]{:S(2)}) async-start(f32[128,16,128]{2,1,0:T(8,128)} %bitcast_select_fusion), calls=%async_computation | async-start | bytes 2097152 | tf_op jit(solution)/shard_map/all_to_all | solution.py:375
  124.3 1.0 copy-start

commit v2 on v1

--- a/solution.py
+++ b/solution.py
@@ -2,7 +2,6 @@
 
 import jax
 import jax.numpy as jnp
-import numpy as np
 from jax import lax
 from jax.experimental import pallas as pl
 from jax.experimental.pallas import tpu as pltpu
@@ -12,6 +11,7 @@
 LEV = 8
 BITREV = (0, 4, 2, 6, 1, 5, 3, 7)
 NACC = 2
+CHUNK = 16
 MESH = pl.DeviceIdType.MESH
 
 
@@ -28,7 +28,9 @@
     return dot(a[0], b[0]) + dot(a[1], b[0]) + dot(a[0], b[1])
 
 
-def grid_kernel(vals_hbm, cells_hbm, mixer, out, edges, vals, cells_v, cells_t, cells, table, sems, *grids):
+def grid_kernel(vals_hbm, cells_hbm, mixer, out, edges, vals, cells_v, cells_t, cells, table, sems, ga, gb, ha0, ha1, hb0, hb1):
+    grids = (ga, gb)
+    half1, half2 = (ha0, ha1), (hb0, hb1)
     copies = [
         pltpu.make_async_copy(vals_hbm.at[pl.ds(q * 32, 32)], vals.at[pl.ds(q * 32, 32)], sems.at[q])
         for q in range(4)
@@ -85,9 +87,12 @@
     b2 = (lane8 & 4) == 0
     packed = table
 
-    def gather(t, carry):
-        for u in range(2):
-            base = t * 16 + u * 8
+    def swap(keep, a, b, shift):
+        return jnp.where(keep, a, b) + pltpu.roll(jnp.where(keep, b, a), shift, 1)
+
+    def first(chunk, to):
+        for s in range(CHUNK):
+            base = chunk * (8 * CHUNK) + s * 8
             a = []
             for q in range(8):
                 off = pl.multiple_of(BITREV[q] * 4096 + base, 8)
@@ -95,19 +100,29 @@
                 for grid in grids[1:]:
                     x = x + grid[pl.ds(off, 8), :]
                 a.append(x)
-            b = [
-                jnp.where(b0, a[q], a[q + 4]) + pltpu.roll(jnp.where(b0, a[q + 4], a[q]), 16, 1)
-                for q in range(4)
-            ]
-            c = [
-                jnp.where(b1, b[q], b[q + 2]) + pltpu.roll(jnp.where(b1, b[q + 2], b[q]), 32, 1)
-                for q in range(2)
-            ]
-            d = jnp.where(b2, c[0], c[1]) + pltpu.roll(jnp.where(b2, c[1], c[0]), 64, 1)
-            packed[pl.ds(pl.multiple_of(base, 8), 8), :] = d
-        return carry
-
-    lax.fori_loop(0, 256, gather, 0)
+            for q in range(4):
+                to[s * 4 + q] = swap(b0, a[q], a[q + 4], 16)
+
+    def second(src, to):
+        for s in range(CHUNK):
+            for q in range(2):
+                to[s * 2 + q] = swap(b1, src[s * 4 + q], src[s * 4 + q + 2], 32)
+
+    def third(src, chunk):
+        for s in range(CHUNK):
+            base = pl.multiple_of(chunk * (8 * CHUNK) + s * 8, 8)
+            packed[pl.ds(base, 8), :] = swap(b2, src[s * 2], src[s * 2 + 1], 64)
+
+    def gather(t, carry):
+        last = 4096 // (8 * CHUNK) - 1
+        for u in range(2):
+            chunk = t * 2 + u
+            third(half2[u], jnp.maximum(chunk - 2, 0))
+            second(half1[1 - u], half2[1 - u])
+            first(jnp.minimum(chunk, last), half1[u])
+        return carry
+
+    lax.fori_loop(0, 2048 // (8 * CHUNK) + 1, gather, 0)
 
     def turn(k2, carry):
         for cb in range(4):
@@ -155,14 +170,13 @@
             pltpu.VMEM((4096, 128), jnp.float32),
             pltpu.SemaphoreType.DMA((6,)),
         ]
-        + [pltpu.VMEM((32768, 128), jnp.float32)] * NACC,
+        + [pltpu.VMEM((32768, 128), jnp.float32)] * NACC
+        + [pltpu.VMEM((4 * CHUNK, 8, 128), jnp.float32)] * 2
+        + [pltpu.VMEM((2 * CHUNK, 8, 128), jnp.float32)] * 2,
         compiler_params=pltpu.CompilerParams(vmem_limit_bytes=60 * 2**20),
         cost_estimate=pl.CostEstimate(flops=10**9, bytes_accessed=4 * 2**20, transcendentals=0),
         name="scatter",
     )(vals, cells, mixer)
-
-
-ROWS = np.concatenate([[base + rg * 8 + k2 for k2 in range(8) for rg in range(4)] for base in (0, 32, -32, 64)])
 
 
 def filter_kernel(n_lat, n_lon, x_hbm, e_hbm, thi, tlo, whi, wlo, ahi, alo, out, x, e, y, send, recv, local):
@@ -335,50 +349,133 @@
     )(x, e, *weights)
 
 
-def band_weights(lengths, weights):
-    def profile(offset):
-        t = offset.astype(np.float32)
-        shape = (2,) + (1,) * t.ndim
+def route_kernel(n_lat, n_lon, obs, cell_in, counts, lengths, weights, mix,
+                 vals, cells, mixer, thi, tlo, whi, wlo, ahi, alo, box, sems):
+    lat = lax.axis_index("lat")
+    lon = lax.axis_index("lon")
+    me = lat * n_lon + lon
+    count = n_lat * n_lon
+    slot = lax.broadcasted_iota(jnp.int32, (16, 128), 1)
+
+    def load(d):
+        box[d] = jnp.where(slot < counts[0, d], obs[d], 0.0)
+
+    def send(k, carry):
+        to_lat = lax.rem(lat + k // n_lon, n_lat)
+        to_lon = lax.rem(lon + lax.rem(k, n_lon), n_lon)
+        d = to_lat * n_lon + to_lon
+        load(d)
+        pltpu.make_async_remote_copy(
+            src_ref=cell_in.at[d], dst_ref=cells.at[me], send_sem=sems.at[0], recv_sem=sems.at[1],
+            device_id=(to_lat, to_lon), device_id_type=MESH,
+        ).start()
+        pltpu.make_async_remote_copy(
+            src_ref=box.at[d], dst_ref=vals.at[me], send_sem=sems.at[2], recv_sem=sems.at[3],
+            device_id=(to_lat, to_lon), device_id_type=MESH,
+        ).start()
+        return carry
+
+    lax.fori_loop(1, count, send, 0)
+    load(me)
+    mine = [
+        pltpu.make_async_copy(cell_in.at[me], cells.at[me], sems.at[4]),
+        pltpu.make_async_copy(box.at[me], vals.at[me], sems.at[5]),
+    ]
+    for copy in mine:
+        copy.start()
+
+    def profile(v, offset):
+        t = offset.astype(jnp.float32)
         total = 0.0
-        for s in range(lengths.shape[1]):
-            scale = t[None] / lengths[:, s].reshape(shape)
-            total = total + weights[:, s].reshape(shape) * jnp.exp(-0.5 * scale**2)
-        return jnp.where(np.abs(offset)[None] <= HALF, total, 0.0)
-
-    taps = profile(np.arange(-HALF, HALF + 1))
-    norm = lax.rsqrt(jnp.sum(taps * taps, axis=1))
-
-    def band(offset):
-        x = profile(offset) * norm.reshape((2,) + (1,) * offset.ndim)
-        hi = lax.reduce_precision(x, 8, 7)
-        return hi.astype(jnp.bfloat16), (x - hi).astype(jnp.bfloat16)
-
-    c = np.arange(512)
-    centre = band(c[:, None] - c[None, :])
-    lane = np.arange(128)
-    kq, t = lane // 32, lane % 32
-    same = kq[:, None, None] == np.arange(4)[None, :, None]
-    col = np.arange(128)[None, None, :]
-    far = 10 * HALF
-    left = np.where(same, (t - 32)[:, None, None] - col, far)
-    right = np.where(same, (t + 128)[:, None, None] - col, far)
-    rims = band(np.stack([left, right]).reshape(2, 128, 512))
-    down = band(ROWS[None, :] - np.arange(64)[:, None])
-    return centre + rims + down
+        for s in range(3):
+            scale = t / lengths[v, s]
+            total = total + weights[v, s] * jnp.exp(-0.5 * (scale * scale))
+        return jnp.where(jnp.abs(offset) <= HALF, total, 0.0)
+
+    def iota(shape, dim):
+        return lax.broadcasted_iota(jnp.int32, shape, dim)
+
+    taps_at = iota((8, 128), 1) - HALF
+    for v in range(2):
+        taps = profile(v, taps_at)
+        norm = lax.rsqrt(jnp.sum(taps * taps, axis=1, keepdims=True))[0:1, 0:1]
+
+        def centre(i, carry):
+            row = iota((32, 512), 0) + i * 32
+            at = pl.ds(pl.multiple_of(i * 32, 32), 32)
+            thi[v, at], tlo[v, at] = split(profile(v, row - iota((32, 512), 1)) * norm)
+            return carry
+
+        lax.fori_loop(0, 16, centre, 0)
+
+        def rim(i, carry):
+            for side, start in enumerate((-32, 128)):
+                offset = iota((32, 512), 0) + start - lax.rem(iota((32, 512), 1), 128)
+                x = jnp.where(iota((32, 512), 1) // 128 == i, profile(v, offset) * norm, 0.0)
+                at = pl.ds(pl.multiple_of(i * 32, 32), 32)
+                whi[v, side, at], wlo[v, side, at] = split(x)
+            return carry
+
+        lax.fori_loop(0, 4, rim, 0)
+        k = iota((64, 128), 1)
+        band = k // 32
+        base = jnp.where(band == 0, 0, jnp.where(band == 1, 32, jnp.where(band == 2, -32, 64)))
+        row = base + lax.rem(k, 4) * 8 + lax.rem(k, 32) // 4
+        ahi[v], alo[v] = split(profile(v, row - iota((64, 128), 0)) * norm)
+
+    row, col = iota((16, 128), 0), iota((16, 128), 1)
+    small = jnp.zeros((16, 128), jnp.float32)
+    for v in range(2):
+        for l in range(LEV):
+            for m in range(LEV):
+                here = (row == v * LEV + m) & (lax.rem(col, 16) == v * LEV + l)
+                small = jnp.where(here, mix[v, l, m], small)
+    for i in range(8):
+        mixer[pl.ds(i * 16, 16)] = jnp.where(col // 16 == i, small, 0.0)
+
+    for copy in mine:
+        copy.wait()
+    rest = pl.ds(0, count - 1)
+    pltpu.make_async_copy(cell_in.at[rest], cells.at[rest], sems.at[0]).wait()
+    pltpu.make_async_copy(cells.at[rest], cells.at[rest], sems.at[1]).wait()
+    pltpu.make_async_copy(box.at[rest], vals.at[rest], sems.at[2]).wait()
+    pltpu.make_async_copy(vals.at[rest], vals.at[rest], sems.at[3]).wait()
+
+
+def route(n_lat, n_lon, obs, cells, counts, lengths, weights, mix):
+    n = n_lat * n_lon
+    vmem = pl.BlockSpec(memory_space=pltpu.VMEM)
+    smem = pl.BlockSpec(memory_space=pltpu.SMEM)
+    hbm = pl.BlockSpec(memory_space=pl.ANY)
+    bf16 = jnp.bfloat16
+    return pl.pallas_call(
+        functools.partial(route_kernel, n_lat, n_lon),
+        out_shape=(
+            jax.ShapeDtypeStruct((n, 16, 128), jnp.float32),
+            jax.ShapeDtypeStruct((n, 1, 128), jnp.int32),
+            jax.ShapeDtypeStruct((128, 128), jnp.float32),
+        )
+        + (jax.ShapeDtypeStruct((2, 512, 512), bf16),) * 2
+        + (jax.ShapeDtypeStruct((2, 2, 128, 512), bf16),) * 2
+        + (jax.ShapeDtypeStruct((2, 64, 128), bf16),) * 2,
+        in_specs=[vmem, hbm, smem, smem, smem, smem],
+        out_specs=[hbm, hbm] + [vmem] * 7,
+        scratch_shapes=[pltpu.VMEM((n, 16, 128), jnp.float32), pltpu.SemaphoreType.DMA((6,))],
+        compiler_params=pltpu.CompilerParams(vmem_limit_bytes=32 * 2**20, has_side_effects=True),
+        cost_estimate=pl.CostEstimate(flops=10**7, bytes_accessed=4 * 2**20, transcendentals=0),
+        name="route",
+    )(obs, cells, counts, lengths, weights, mix)
 
 
 def local(obs_values, obs_cells, obs_counts, filter_lengths, filter_weights, vertical_mix):
-    live = jnp.arange(128)[None, :] < obs_counts[0][:, None]
-    vals = jnp.where(live[:, None, :], obs_values[0].reshape(128, 16, 128), 0.0)
-    axes = ("lat", "lon")
-    cells = lax.all_to_all(obs_cells[0], axes, split_axis=0, concat_axis=0, tiled=True)
-    vals = lax.all_to_all(vals, axes, split_axis=0, concat_axis=0, tiled=True)
-    eye = jnp.eye(8, dtype=jnp.float32)
-    both = jnp.einsum("vlm,vw->vmwl", vertical_mix, jnp.eye(2, dtype=jnp.float32), precision=lax.Precision.HIGHEST)
-    mixer = (eye[:, None, :, None] * both.reshape(16, 16)[None, :, None, :]).reshape(128, 128)
-    weights = band_weights(filter_lengths, filter_weights)
-    x, e = grid_tile(vals, cells, mixer)
-    return filter_tile(lax.axis_size("lat"), lax.axis_size("lon"), x.reshape(2, 2, 256, 512), e, weights)
+    n_lat, n_lon = lax.axis_size("lat"), lax.axis_size("lon")
+    n = n_lat * n_lon
+    vals, cells, mixer, *weights = route(
+        n_lat, n_lon, obs_values.reshape(n, 16, 128), obs_cells.reshape(n, 1, 128), obs_counts,
+        filter_lengths, filter_weights, vertical_mix,
+    )
+    x, e = grid_tile(vals, cells.reshape(128, 128), mixer)
+    return filter_tile(n_lat, n_lon, x.reshape(2, 2, 256, 512), e, weights)
 
 
 def solution(mesh):

time: 153 us -> 92.4 us (0.60)
  Pallas kernels: 105 us -> 82.7 us
  starting transfers between devices: 19.5 us -> 0 us
  waiting for transfers between devices: 14.2 us -> 0 us
  other arithmetic: 8.23 us -> 0 us
  local copies, waits for them, and re-layouts: 6.07 us -> 9.23 us
    pallas_call x1, Pallas kernels: 78.4 us -> 27.8 us  [grid_tile(): pl.pallas_call(grid_kernel, out_shape=(jax.ShapeDtypeStruct((2, 2, 8, 4,...]
    pallas_call x0 -> x1, Pallas kernels: none -> 28.6 us  [route(): pl.pallas_call(functools.partial(route_kernel, n_lat, n_lon), out_shape=(...]
    all_to_all x2 -> x0, starting transfers between devices: 19.5 us -> none  [the longest x1 10.2 us: local(): lax.all_to_all(obs_cells[0], axes, split_axis=0, concat_axis=0, tiled=True)]
    all_to_all x2 -> x0, waiting for transfers between devices: 14.2 us -> none  [the longest x1 13.2 us: local(): vals = lax.all_to_all(vals, axes, split_axis=0, concat_axis=0, tiled=True)]
    unnamed x22 -> x21, local copies, waits for them, and re-layouts: 4.13 us -> 9.23 us
    convert_element_type x4 -> x0, other arithmetic: 4.12 us -> none  [the longest x3 4.12 us: band(): return (hi.astype(jnp.bfloat16), (x - hi).astype(jnp.bfloat16))]
    select_n x1 -> x0, other arithmetic: 2.33 us -> none  [local(): vals = jnp.where(live[:, None, :], obs_values[0].reshape(128, 16, 128), 0.0)]
  transfers between devices with their start and end apart: 2 -> 0, of which waited for: 2 -> 0; matrix products, arithmetic and copies ran while one was open for 8% -> 0% of each run, Pallas kernels for 0% -> 0%
where the time goes in v2:
time: 92.4 us; the launch traced here: 92 us
  Pallas kernels  82.7 us (90%)
  local copies, waits for them, and re-layouts  9.23 us (10%)
    pallas_call x1, Pallas kernels, route(): pl.pallas_call(functools.partial(route_kernel, n_lat, n_lon), out_shape=(...  28.6 us
    pallas_call x1, Pallas kernels, grid_tile(): pl.pallas_call(grid_kernel, out_shape=(jax.ShapeDtypeStruct((2, 2, 8, 4,...  27.8 us
    pallas_call x1, Pallas kernels, filter_tile(): pl.pallas_call(functools.partial(filter_kernel, n_lat, n_lon), out_shape=...  26.3 us
    unnamed x21, local copies, waits for them, and re-layouts  9.23 us

profile of v2, /device:TPU:32, one launch (start us, length us, event | category | flops | bytes accessed | tf_op | source)
XLA Modules:
  0.0 92.0 jit_solution(7949978969230809267)
XLA Ops:
  0.0 0.0 copy-start
  0.0 1.2 %copy-done = f32[1,128,2,8,128]{4,3,2,1,0:T(8,128)S(1)} copy-done((f32[1,128,2,8,128]{4,3,2,1,0:T(8,128)S(1)}, f32[1,128,2,8,128]{4,3,2,1,0:T(8,128)}, u32[]{:S(2)}) %copy-start) | copy-done | bytes 1048600
  1.2 0.0 copy-start.1
  1.2 0.8 copy-done.1
  2.1 0.0 copy-start.2
  2.1 0.7 copy-done.2
  2.8 0.0 copy-start.3
  2.8 0.7 copy-done.3
  3.4 0.0 copy-start.4
  3.4 0.7 copy-done.4
  4.1 0.0 copy-start.5
  4.1 0.7 copy-done.5
  4.8 28.6 %route.1 = (f32[128,16,128]{2,1,0:T(8,128)S(1)}, s32[128,1,128]{2,1,0:T(1,128)S(1)}, f32[128,128]{1,0:T(8,128)S(1)}, bf16[2,512,512]{2,1,0:T(8,128)(2,1)S(1)}, b...) custom-call(f32[128,16,128]{2,1,0:T(8,128)S(1)} %bitcast.4, ...), custom_call_target="tpu_custom_call" | custom-call | flops 10000000 | bytes 4194304 | tf_op jit(solution)/shard_map/route/pallas_call | solution.py:451
  33.4 0.0 copy-start.6
  33.4 1.0 %copy-done.6 = f32[128,16,128]{2,1,0:T(8,128)} copy-done((f32[128,16,128]{2,1,0:T(8,128)}, f32[128,16,128]{2,1,0:T(8,128)S(1)}, u32[]{:S(2)}) %copy-start.6) | copy-done | bytes 1048600
  34.4 0.0 copy-start.7
  34.4 0.6 copy-done.7
  35.0 0.0 copy-start.8
  35.0 0.6 copy-done.8
  35.6 27.8 %scatter.1 = (f32[2,2,8,4,8,512]{5,4,3,2,1,0:T(8,128)}, f32[2,2,2,64,128]{4,3,2,1,0:T(8,128)}) custom-call(f32[128,16,128]{2,1,0:T(8,128)} %copy-done.6, s32[128,128]{1,0:T(8,128)} %bitcast.6, f32[128,128]{1,0:T(8,128)} %copy-done.8), custom_call_target="tpu_custom_call" | custom-call | flops 1000000000 | bytes 4194304 | tf_op jit(solution)/shard_map/scatter/pallas_call | solution.py:153
  63.4 0.0 copy-start.9
  63.4 0.9 %copy-done.9 = f32[2,2,2,64,128]{4,3,2,1,0:T(8,128)S(1)} copy-done((f32[2,2,2,64,128]{4,3,2,1,0:T(8,128)S(1)}, f32[2,2,2,64,128]{4,3,2,1,0:T(8,128)}, u32[]{:S(2)}) %copy-start.9) | copy-done | bytes 262168
  64.4 26.3 %filters.1 = f32[2,8,64,512]{3,2,1,0:T(8,128)S(1)} custom-call(f32[2,2,256,512]{3,2,1,0:T(8,128)} %bitcast.7, f32[2,2,2,64,128]{4,3,2,1,0:T(8,128)S(1)} %copy-done.9, bf16[2,512,512]{2,1,0:T(8,128)(2,1)S(1)} %get-tuple-element.21.thi, bf16[2,512,512]{2,1,0:T(8,128)(2,1)S(1)} %get-tuple-element.22.tlo, bf16[2,2,128,512]{3,2,1,0:T(8,128)(2,1)S(1)} %get-tuple-element.23.whi, ...), custom_call_target="tpu_custom_call" | custom-call | flops 6000000000 | bytes 8388608 | tf_op jit(solution)/shard_map/filters/pallas_call | solution.py:331
  90.7 1.3 %copy.8 = f32[2,8,64,512]{3,2,1,0:T(8,128)} copy(f32[2,8,64,512]{3,2,1,0:T(8,128)S(1)} %filters.1) | data formatting | bytes 4194304
Async XLA Ops:
  0.0 1.2 %copy-start = (f32[1,128,2,8,128]{4,3,2,1,0:T(8,128)S(1)}, f32[1,128,2,8,128]{4,3,2,1,0:T(8,128)}, u32[]{:S(2)}) copy-start(f32[1,128,2,8,128]{4,3,2,1,0:T(8,128)} %param.6) | copy-start | bytes 3145732
  1.2 0.8 copy-start.1
  2.1 0.7 copy-start.2
  2.8 0.7 copy-start.3
  3.4 0.7 copy-start.4
  4.1 0.7 copy-start.5
  33.4 1.0 %copy-start.6 = (f32[128,16,128]{2,1,0:T(8,128)}, f32[128,16,128]{2,1,0:T(8,128)S(1)}, u32[]{:S(2)}) copy-start(f32[128,16,128]{2,1,0:T(8,128)S(1)} %get-tuple-element.16.vals_hbm) | copy-start | bytes 3145732
  34.4 0.6 copy-start.7
  35.0 0.6 copy-start.8
  63.4 1.0 %copy-start.9 = (f32[2,2,2,64,128]{4,3,2,1,0:T(8,128)S(1)}, f32[2,2,2,64,128]{4,3,2,1,0:T(8,128)}, u32[]{:S(2)}) copy-start(f32[2,2,2,64,128]{4,3,2,1,0:T(8,128)} %get-tuple-element.20.e_hbm) | copy-start | bytes 786436

commit v3 on v2

--- a/solution.py
+++ b/solution.py
@@ -12,6 +12,7 @@
 BITREV = (0, 4, 2, 6, 1, 5, 3, 7)
 NACC = 2
 CHUNK = 16
+VMEM = 62 * 2**20
 MESH = pl.DeviceIdType.MESH
 
 
@@ -28,21 +29,15 @@
     return dot(a[0], b[0]) + dot(a[1], b[0]) + dot(a[0], b[1])
 
 
-def grid_kernel(vals_hbm, cells_hbm, mixer, out, edges, vals, cells_v, cells_t, cells, table, sems, ga, gb, ha0, ha1, hb0, hb1):
+def grid_kernel(table_hbm, cells_hbm, out_hbm, edges, table, cells, out, sems, ga, gb, ha0, ha1, hb0, hb1):
     grids = (ga, gb)
     half1, half2 = (ha0, ha1), (hb0, hb1)
-    copies = [
-        pltpu.make_async_copy(vals_hbm.at[pl.ds(q * 32, 32)], vals.at[pl.ds(q * 32, 32)], sems.at[q])
-        for q in range(4)
+    loads = [
+        pltpu.make_async_copy(table_hbm, table.at[pl.ds(0, 2048)], sems.at[0]),
+        pltpu.make_async_copy(cells_hbm, cells, sems.at[1]),
     ]
-    cell_copy = pltpu.make_async_copy(cells_hbm, cells_v, sems.at[4])
-    cell_copy.start()
-    for copy in copies:
+    for copy in loads:
         copy.start()
-    cell_copy.wait()
-    cells_t[...] = cells_v[...].T
-    to_smem = pltpu.make_async_copy(cells_t, cells, sems.at[5])
-    to_smem.start()
 
     def clear(i, carry):
         for grid in grids:
@@ -50,21 +45,10 @@
         return carry
 
     lax.fori_loop(0, 32768 // 256, clear, 0)
-    mix = split(mixer[...])
-    for copy in copies:
-        copy.wait()
-
-    def mix_rows(step, carry):
-        for u in range(4):
-            sg = step * 4 + u
-            v = vals[pl.ds(pl.multiple_of(sg * 8, 8), 8)].reshape(128, 128).T
-            table[pl.ds(pl.multiple_of(sg * 128, 128), 128), :] = dot3(split(v), mix)
-        return carry
-
-    lax.fori_loop(0, 4, mix_rows, 0)
     lane = lax.broadcasted_iota(jnp.int32, (1, 128), 1) // 16
     masks = [lane == i for i in range(8)]
-    to_smem.wait()
+    for copy in loads:
+        copy.wait()
 
     def scatter(j, carry):
         for g0 in range(0, 16, NACC):
@@ -134,6 +118,8 @@
         return carry
 
     lax.fori_loop(0, 8, turn, 0)
+    write = pltpu.make_async_copy(out, out_hbm, sems.at[2])
+    write.start()
 
     quarter = lax.broadcasted_iota(jnp.int32, (32, 128), 1) // 32
     for h in range(2):
@@ -147,39 +133,35 @@
                         x = pltpu.roll(x, shift, 1) if shift else x
                         total = x if total is None else jnp.where(quarter == kq, x, total)
                     edges[side, h, v, pl.ds(kk * 32, 32), :] = total
-
-
-def grid_tile(vals, cells, mixer):
+    write.wait()
+
+
+def grid_tile(table, cells):
+    hbm = pl.BlockSpec(memory_space=pl.ANY)
     return pl.pallas_call(
         grid_kernel,
         out_shape=(
             jax.ShapeDtypeStruct((2, 2, 8, 4, 8, 512), jnp.float32),
             jax.ShapeDtypeStruct((2, 2, 2, 64, 128), jnp.float32),
         ),
-        in_specs=[
-            pl.BlockSpec(memory_space=pl.ANY),
-            pl.BlockSpec(memory_space=pl.ANY),
-            pl.BlockSpec(memory_space=pltpu.VMEM),
-        ],
-        out_specs=[pl.BlockSpec(memory_space=pltpu.VMEM)] * 2,
+        in_specs=[hbm, hbm],
+        out_specs=[hbm, pl.BlockSpec(memory_space=pltpu.VMEM)],
         scratch_shapes=[
-            pltpu.VMEM((128, 16, 128), jnp.float32),
-            pltpu.VMEM((128, 128), jnp.int32),
-            pltpu.VMEM((128, 128), jnp.int32),
+            pltpu.VMEM((4096, 128), jnp.float32),
             pltpu.SMEM((128, 128), jnp.int32),
-            pltpu.VMEM((4096, 128), jnp.float32),
-            pltpu.SemaphoreType.DMA((6,)),
+            pltpu.VMEM((2, 2, 8, 4, 8, 512), jnp.float32),
+            pltpu.SemaphoreType.DMA((3,)),
         ]
         + [pltpu.VMEM((32768, 128), jnp.float32)] * NACC
         + [pltpu.VMEM((4 * CHUNK, 8, 128), jnp.float32)] * 2
         + [pltpu.VMEM((2 * CHUNK, 8, 128), jnp.float32)] * 2,
-        compiler_params=pltpu.CompilerParams(vmem_limit_bytes=60 * 2**20),
+        compiler_params=pltpu.CompilerParams(vmem_limit_bytes=VMEM),
         cost_estimate=pl.CostEstimate(flops=10**9, bytes_accessed=4 * 2**20, transcendentals=0),
         name="scatter",
-    )(vals, cells, mixer)
-
-
-def filter_kernel(n_lat, n_lon, x_hbm, e_hbm, thi, tlo, whi, wlo, ahi, alo, out, x, e, y, send, recv, local):
+    )(table, cells)
+
+
+def filter_kernel(n_lat, n_lon, x_hbm, e_hbm, t_hbm, w_hbm, a_hbm, out, x, e, y, t, w, a, send, recv, local):
     lat = lax.axis_index("lat")
     lon = lax.axis_index("lon")
     west = lax.rem(lon + n_lon - 1, n_lon)
@@ -190,7 +172,14 @@
     has_south = lat < n_lat - 1
 
     own_x = pltpu.make_async_copy(x_hbm, x.at[pl.ds(0, 2)], local.at[0])
-    own_x.start()
+    loads = [
+        own_x,
+        pltpu.make_async_copy(t_hbm, t, local.at[1]),
+        pltpu.make_async_copy(w_hbm, w, local.at[2]),
+        pltpu.make_async_copy(a_hbm, a, local.at[3]),
+    ]
+    for copy in loads:
+        copy.start()
 
     barrier = pltpu.get_barrier_semaphore()
 
@@ -259,18 +248,18 @@
         e[:, 3] = jnp.zeros((2, 2, 64, 128), jnp.float32)
 
     def along_lon(s, v):
-        rows = dot3(split(x[s, v]), (thi[v], tlo[v]))
+        rows = dot3(split(x[s, v]), (t[0, v], t[1, v]))
         for cb in range(4):
             y[s, v, cb] = rows[:, cb * 128 : cb * 128 + 128]
         for side in range(2):
-            rim = dot3(split(e[side, s, v]), (whi[v, side], wlo[v, side]))
+            rim = dot3(split(e[side, s, v]), (w[0, v, side], w[1, v, side]))
             for kk in range(2):
                 for kq in range(4):
                     at = pl.ds((kk * 4 + kq) * 32, 32)
                     y[s, v, side * 3, at] += rim[kk * 32 : kk * 32 + 32, kq * 128 : kq * 128 + 128]
 
     def along_lat(v):
-        a = ahi[v], alo[v]
+        band = a[0, v], a[1, v]
 
         def level(l, carry):
             rows = jnp.concatenate(
@@ -280,12 +269,13 @@
                 ],
                 axis=0,
             )
-            out[v, l] = dot3(a, split(rows))
+            out[v, l] = dot3(band, split(rows))
             return carry
 
         lax.fori_loop(0, LEV, level, 0)
 
-    own_x.wait()
+    for copy in loads:
+        copy.wait()
     for copy in sides:
         copy.wait_recv()
 
@@ -331,58 +321,88 @@
     return pl.pallas_call(
         functools.partial(filter_kernel, n_lat, n_lon),
         out_shape=jax.ShapeDtypeStruct((2, 8, 64, 512), jnp.float32),
-        in_specs=[pl.BlockSpec(memory_space=pl.ANY)] * 2 + [pl.BlockSpec(memory_space=pltpu.VMEM)] * 6,
+        in_specs=[pl.BlockSpec(memory_space=pl.ANY)] * 5,
         out_specs=pl.BlockSpec(memory_space=pltpu.VMEM),
         scratch_shapes=[
             pltpu.VMEM((4, 2, 256, 512), jnp.float32),
             pltpu.VMEM((2, 4, 2, 64, 128), jnp.float32),
             pltpu.VMEM((4, 2, 4, 256, 128), jnp.float32),
+            pltpu.VMEM((2, 2, 512, 512), jnp.bfloat16),
+            pltpu.VMEM((2, 2, 2, 128, 512), jnp.bfloat16),
+            pltpu.VMEM((2, 2, 64, 128), jnp.bfloat16),
             pltpu.SemaphoreType.DMA((10,)),
             pltpu.SemaphoreType.DMA((10,)),
-            pltpu.SemaphoreType.DMA((1,)),
+            pltpu.SemaphoreType.DMA((4,)),
         ],
         compiler_params=pltpu.CompilerParams(
-            vmem_limit_bytes=48 * 2**20, collective_id=0, has_side_effects=True
+            vmem_limit_bytes=VMEM, collective_id=0, has_side_effects=True
         ),
         cost_estimate=pl.CostEstimate(flops=6 * 10**9, bytes_accessed=8 * 2**20, transcendentals=0),
         name="filters",
     )(x, e, *weights)
 
 
-def route_kernel(n_lat, n_lon, obs, cell_in, counts, lengths, weights, mix,
-                 vals, cells, mixer, thi, tlo, whi, wlo, ahi, alo, box, sems):
+def route_kernel(n_lat, n_lon, obs_hbm, cells_hbm, counts_hbm, lengths_hbm, weights_hbm, mix_hbm,
+                 table, cells_out, t_out, w_out, a_out,
+                 box, cell_box, vals, cells, counts, lengths, weights, mix, tiles, local, send, recv):
     lat = lax.axis_index("lat")
     lon = lax.axis_index("lon")
     me = lat * n_lon + lon
     count = n_lat * n_lon
+
+    loads = [
+        pltpu.make_async_copy(src, dst, local.at[i])
+        for i, (src, dst) in enumerate(
+            ((obs_hbm, box), (cells_hbm, cell_box), (counts_hbm, counts), (lengths_hbm, lengths),
+             (weights_hbm, weights), (mix_hbm, mix))
+        )
+    ]
+    for copy in loads:
+        copy.start()
+
+    barrier = pltpu.get_barrier_semaphore()
+
+    def peer(k):
+        return lax.rem(lat + k // n_lon, n_lat), lax.rem(lon + lax.rem(k, n_lon), n_lon)
+
+    def greet(k, carry):
+        pl.semaphore_signal(barrier, inc=1, device_id=peer(k), device_id_type=MESH)
+        return carry
+
+    lax.fori_loop(1, count, greet, 0)
+    for copy in loads:
+        copy.wait()
+
     slot = lax.broadcasted_iota(jnp.int32, (16, 128), 1)
 
-    def load(d):
-        box[d] = jnp.where(slot < counts[0, d], obs[d], 0.0)
-
-    def send(k, carry):
-        to_lat = lax.rem(lat + k // n_lon, n_lat)
-        to_lon = lax.rem(lon + lax.rem(k, n_lon), n_lon)
+    def mask(i, carry):
+        for u in range(8):
+            d = i * 8 + u
+            box[d] = jnp.where(slot < counts[0, d], box[d], 0.0)
+        return carry
+
+    lax.fori_loop(0, count // 8, mask, 0)
+    pl.semaphore_wait(barrier, count - 1)
+
+    def to(k, carry):
+        to_lat, to_lon = peer(k)
         d = to_lat * n_lon + to_lon
-        load(d)
         pltpu.make_async_remote_copy(
-            src_ref=cell_in.at[d], dst_ref=cells.at[me], send_sem=sems.at[0], recv_sem=sems.at[1],
+            src_ref=cell_box.at[d], dst_ref=cells.at[me], send_sem=send.at[0], recv_sem=recv.at[n_lat],
             device_id=(to_lat, to_lon), device_id_type=MESH,
         ).start()
         pltpu.make_async_remote_copy(
-            src_ref=box.at[d], dst_ref=vals.at[me], send_sem=sems.at[2], recv_sem=sems.at[3],
+            src_ref=box.at[d], dst_ref=vals.at[me], send_sem=send.at[1], recv_sem=recv.at[lat],
             device_id=(to_lat, to_lon), device_id_type=MESH,
         ).start()
         return carry
 
-    lax.fori_loop(1, count, send, 0)
-    load(me)
-    mine = [
-        pltpu.make_async_copy(cell_in.at[me], cells.at[me], sems.at[4]),
-        pltpu.make_async_copy(box.at[me], vals.at[me], sems.at[5]),
-    ]
-    for copy in mine:
-        copy.start()
+    lax.fori_loop(1, count, to, 0)
+    pltpu.make_async_copy(cell_box.at[me], cells.at[me], recv.at[n_lat]).start()
+    pltpu.make_async_copy(box.at[me], vals.at[me], recv.at[lat]).start()
+
+    def iota(shape, dim):
+        return lax.broadcasted_iota(jnp.int32, shape, dim)
 
     def profile(v, offset):
         t = offset.astype(jnp.float32)
@@ -392,36 +412,30 @@
             total = total + weights[v, s] * jnp.exp(-0.5 * (scale * scale))
         return jnp.where(jnp.abs(offset) <= HALF, total, 0.0)
 
-    def iota(shape, dim):
-        return lax.broadcasted_iota(jnp.int32, shape, dim)
-
-    taps_at = iota((8, 128), 1) - HALF
+    flat = (128, 128)
     for v in range(2):
-        taps = profile(v, taps_at)
+        taps = profile(v, iota((8, 128), 1) - HALF)
         norm = lax.rsqrt(jnp.sum(taps * taps, axis=1, keepdims=True))[0:1, 0:1]
-
-        def centre(i, carry):
-            row = iota((32, 512), 0) + i * 32
-            at = pl.ds(pl.multiple_of(i * 32, 32), 32)
-            thi[v, at], tlo[v, at] = split(profile(v, row - iota((32, 512), 1)) * norm)
-            return carry
-
-        lax.fori_loop(0, 16, centre, 0)
-
-        def rim(i, carry):
-            for side, start in enumerate((-32, 128)):
-                offset = iota((32, 512), 0) + start - lax.rem(iota((32, 512), 1), 128)
-                x = jnp.where(iota((32, 512), 1) // 128 == i, profile(v, offset) * norm, 0.0)
-                at = pl.ds(pl.multiple_of(i * 32, 32), 32)
-                whi[v, side, at], wlo[v, side, at] = split(x)
-            return carry
-
-        lax.fori_loop(0, 4, rim, 0)
+        for i in range(3):
+            hi, lo = split(profile(v, iota(flat, 0) - iota(flat, 1) + (i - 1) * 128) * norm)
+            tiles[0, i] = hi
+            tiles[1, i] = lo
+        blank = jnp.zeros(flat, jnp.bfloat16)
+        for p in range(2):
+            for i in range(4):
+                for j in range(4):
+                    piece = tiles[p, i - j + 1] if abs(i - j) <= 1 else blank
+                    t_out[p, v, pl.ds(i * 128, 128), pl.ds(j * 128, 128)] = piece
+            w_out[p, v] = jnp.zeros((2, 128, 512), jnp.bfloat16)
+            for kq in range(4):
+                at = pl.ds(kq * 32, 32), pl.ds(kq * 128, 128)
+                w_out[(p, v, 0) + at] = tiles[p, 0, pl.ds(96, 32)]
+                w_out[(p, v, 1) + at] = tiles[p, 2, pl.ds(0, 32)]
         k = iota((64, 128), 1)
         band = k // 32
         base = jnp.where(band == 0, 0, jnp.where(band == 1, 32, jnp.where(band == 2, -32, 64)))
         row = base + lax.rem(k, 4) * 8 + lax.rem(k, 32) // 4
-        ahi[v], alo[v] = split(profile(v, row - iota((64, 128), 0)) * norm)
+        a_out[0, v], a_out[1, v] = split(profile(v, row - iota((64, 128), 0)) * norm)
 
     row, col = iota((16, 128), 0), iota((16, 128), 1)
     small = jnp.zeros((16, 128), jnp.float32)
@@ -430,38 +444,54 @@
             for m in range(LEV):
                 here = (row == v * LEV + m) & (lax.rem(col, 16) == v * LEV + l)
                 small = jnp.where(here, mix[v, l, m], small)
-    for i in range(8):
-        mixer[pl.ds(i * 16, 16)] = jnp.where(col // 16 == i, small, 0.0)
-
-    for copy in mine:
-        copy.wait()
+    mixer = split(jnp.concatenate([jnp.where(col // 16 == i, small, 0.0) for i in range(8)], axis=0))
+
+    def group(i, carry):
+        g = lax.rem(lat + n_lat - i, n_lat)
+        here = pl.ds(pl.multiple_of(g * 8, 8), 8)
+        pltpu.make_async_copy(vals.at[here], vals.at[here], recv.at[g]).wait()
+        rows = vals[here].reshape(128, 128).T
+        table[pl.ds(pl.multiple_of(g * 128, 128), 128), :] = dot3(split(rows), mixer)
+        return carry
+
+    lax.fori_loop(0, n_lat, group, 0)
+    pltpu.make_async_copy(cells, cells, recv.at[n_lat]).wait()
+    cells_out[...] = cells[:, 0, :].T
     rest = pl.ds(0, count - 1)
-    pltpu.make_async_copy(cell_in.at[rest], cells.at[rest], sems.at[0]).wait()
-    pltpu.make_async_copy(cells.at[rest], cells.at[rest], sems.at[1]).wait()
-    pltpu.make_async_copy(box.at[rest], vals.at[rest], sems.at[2]).wait()
-    pltpu.make_async_copy(vals.at[rest], vals.at[rest], sems.at[3]).wait()
+    pltpu.make_async_copy(cell_box.at[rest], cells.at[rest], send.at[0]).wait()
+    pltpu.make_async_copy(box.at[rest], vals.at[rest], send.at[1]).wait()
 
 
 def route(n_lat, n_lon, obs, cells, counts, lengths, weights, mix):
     n = n_lat * n_lon
-    vmem = pl.BlockSpec(memory_space=pltpu.VMEM)
-    smem = pl.BlockSpec(memory_space=pltpu.SMEM)
     hbm = pl.BlockSpec(memory_space=pl.ANY)
     bf16 = jnp.bfloat16
     return pl.pallas_call(
         functools.partial(route_kernel, n_lat, n_lon),
         out_shape=(
-            jax.ShapeDtypeStruct((n, 16, 128), jnp.float32),
-            jax.ShapeDtypeStruct((n, 1, 128), jnp.int32),
-            jax.ShapeDtypeStruct((128, 128), jnp.float32),
-        )
-        + (jax.ShapeDtypeStruct((2, 512, 512), bf16),) * 2
-        + (jax.ShapeDtypeStruct((2, 2, 128, 512), bf16),) * 2
-        + (jax.ShapeDtypeStruct((2, 64, 128), bf16),) * 2,
-        in_specs=[vmem, hbm, smem, smem, smem, smem],
-        out_specs=[hbm, hbm] + [vmem] * 7,
-        scratch_shapes=[pltpu.VMEM((n, 16, 128), jnp.float32), pltpu.SemaphoreType.DMA((6,))],
-        compiler_params=pltpu.CompilerParams(vmem_limit_bytes=32 * 2**20, has_side_effects=True),
+            jax.ShapeDtypeStruct((n * 16, 128), jnp.float32),
+            jax.ShapeDtypeStruct((n, 128), jnp.int32),
+            jax.ShapeDtypeStruct((2, 2, 512, 512), bf16),
+            jax.ShapeDtypeStruct((2, 2, 2, 128, 512), bf16),
+            jax.ShapeDtypeStruct((2, 2, 64, 128), bf16),
+        ),
+        in_specs=[hbm] * 6,
+        out_specs=[pl.BlockSpec(memory_space=pltpu.VMEM)] * 5,
+        scratch_shapes=[
+            pltpu.VMEM((n, 16, 128), jnp.float32),
+            pltpu.VMEM((n, 1, 128), jnp.int32),
+            pltpu.VMEM((n, 16, 128), jnp.float32),
+            pltpu.VMEM((n, 1, 128), jnp.int32),
+            pltpu.SMEM((1, n), jnp.int32),
+            pltpu.SMEM((2, 3), jnp.float32),
+            pltpu.SMEM((2, 3), jnp.float32),
+            pltpu.SMEM((2, LEV, LEV), jnp.float32),
+            pltpu.VMEM((2, 3, 128, 128), bf16),
+            pltpu.SemaphoreType.DMA((6,)),
+            pltpu.SemaphoreType.DMA((2,)),
+            pltpu.SemaphoreType.DMA((n_lat + 1,)),
+        ],
+        compiler_params=pltpu.CompilerParams(vmem_limit_bytes=VMEM, collective_id=1, has_side_effects=True),
         cost_estimate=pl.CostEstimate(flops=10**7, bytes_accessed=4 * 2**20, transcendentals=0),
         name="route",
     )(obs, cells, counts, lengths, weights, mix)
@@ -470,11 +500,11 @@
 def local(obs_values, obs_cells, obs_counts, filter_lengths, filter_weights, vertical_mix):
     n_lat, n_lon = lax.axis_size("lat"), lax.axis_size("lon")
     n = n_lat * n_lon
-    vals, cells, mixer, *weights = route(
+    table, cells, *weights = route(
         n_lat, n_lon, obs_values.reshape(n, 16, 128), obs_cells.reshape(n, 1, 128), obs_counts,
         filter_lengths, filter_weights, vertical_mix,
     )
-    x, e = grid_tile(vals, cells.reshape(128, 128), mixer)
+    x, e = grid_tile(table, cells)
     return filter_tile(n_lat, n_lon, x.reshape(2, 2, 256, 512), e, weights)
 
 

time: 92.4 us -> 85.7 us (0.927)
  local copies, waits for them, and re-layouts: 9.23 us -> 3.14 us
    unnamed x21 -> x1, local copies, waits for them, and re-layouts: 9.23 us -> 3.14 us
    pallas_call x1, Pallas kernels: 26.3 us -> 29 us  [filter_tile(): pl.pallas_call(functools.partial(filter_kernel, n_lat, n_lon), out_shape=...]
    pallas_call x1, Pallas kernels: 27.8 us -> 25.3 us  [grid_tile(): pl.pallas_call(grid_kernel, out_shape=(jax.ShapeDtypeStruct((2, 2, 8, 4,...]
where the time goes in v3:
time: 85.7 us; the launch traced here: 85.6 us
  Pallas kernels  82.4 us (96%)
  local copies, waits for them, and re-layouts  3.14 us (4%)
    pallas_call x1, Pallas kernels, filter_tile(): pl.pallas_call(functools.partial(filter_kernel, n_lat, n_lon), out_shape=...  29 us
    pallas_call x1, Pallas kernels, route(): pl.pallas_call(functools.partial(route_kernel, n_lat, n_lon), out_shape=(...  28.1 us
    pallas_call x1, Pallas kernels, grid_tile(): pl.pallas_call(grid_kernel, out_shape=(jax.ShapeDtypeStruct((2, 2, 8, 4,...  25.3 us
    unnamed x1, local copies, waits for them, and re-layouts  3.14 us

profile of v3, /device:TPU:32, one launch (start us, length us, event | category | flops | bytes accessed | tf_op | source)
XLA Modules:
  0.0 85.6 jit_solution(4810278976499070395)
XLA Ops:
  0.0 28.1 %route.1 = (f32[2048,128]{1,0:T(8,128)}, s32[128,128]{1,0:T(8,128)}, bf16[2,2,512,512]{3,2,1,0:T(8,128)(2,1)}, bf16[2,2,2,128,512]{4,3,2,1,0:T(8,128)(2,1)}, bf16[2,2,64,128]{3,2,1,0:T(8,128)(2,1)}) custom-call(f32[128,16,128]{2,1,0:T(8,128)} %bitcast.3, s32[128,1,128]{2,1,0:T(1,128)} %bitcast.4, s32[1,128]{1,0:T(1,128)} %counts_hbm.1, f32[2,3]{1,0:T(2,128)} %lengths_hbm.1, ...), custom_call_target="tpu_custom_call" | custom-call | flops 10000000 | bytes 4194304 | tf_op jit(solution)/shard_map/route/pallas_call | solution.py:469
  28.2 25.3 %scatter.1 = (f32[2,2,8,4,8,512]{5,4,3,2,1,0:T(8,128)}, f32[2,2,2,64,128]{4,3,2,1,0:T(8,128)}) custom-call(f32[2048,128]{1,0:T(8,128)} %get-tuple-element.12.table_hbm, s32[128,128]{1,0:T(8,128)} %get-tuple-element.13.cells_hbm), custom_call_target="tpu_custom_call" | custom-call | flops 1000000000 | bytes 4194304 | tf_op jit(solution)/shard_map/scatter/pallas_call | solution.py:141
  53.4 29.0 %filters.1 = f32[2,8,64,512]{3,2,1,0:T(8,128)} custom-call(f32[2,2,256,512]{3,2,1,0:T(8,128)} %bitcast.5, f32[2,2,2,64,128]{4,3,2,1,0:T(8,128)} %get-tuple-element.15.e_hbm, bf16[2,2,512,512]{3,2,1,0:T(8,128)(2,1)} %get-tuple-element.16.t_hbm, bf16[2,2,2,128,512]{4,3,2,1,0:T(8,128)(2,1)} %get-tuple-element.17.w_hbm, ...), custom_call_target="tpu_custom_call" | custom-call | flops 6000000000 | bytes 8388608 | tf_op jit(solution)/shard_map/filters/pallas_call | solution.py:321
  82.5 3.1 %copy.8 = f32[2,8,64,512]{3,2,1,0:T(8,128)} copy(f32[2,8,64,512]{3,2,1,0:T(8,128)} %filters.1) | data formatting | bytes 4194304

commit v4 on v3

v4 whole, which is shorter than its diff:
```python
import functools

import jax
import jax.numpy as jnp
from jax import lax
from jax.experimental import pallas as pl
from jax.experimental.pallas import tpu as pltpu
from jax.sharding import PartitionSpec as P

HALF = 31
LEV = 8
NACC = 2
UNROLL = 2
BLOCKS = 4
VMEM = 62 * 2**20
MESH = pl.DeviceIdType.MESH


def split(x):
    hi = x.astype(jnp.bfloat16)
    return hi, (x - hi.astype(jnp.float32)).astype(jnp.bfloat16)


def dot(a, b):
    return jnp.dot(a, b, preferred_element_type=jnp.float32)


def dot3(a, b):
    return dot(a[0], b[0]) + dot(a[1], b[0]) + dot(a[0], b[1])


def grid_kernel(table_hbm, cells_hbm, out_hbm, table, out, picker, sized, sems, ga, gb, *cells):
    grids = (ga, gb)
    load = pltpu.make_async_copy(table_hbm, table, sems.at[0])
    load.start()
    for s in range(128):
        pltpu.make_async_copy(cells_hbm.at[s, 0], cells[s], sems.at[1]).start()

    def clear(i, carry):
        for grid in grids:
            grid[pl.ds(pl.multiple_of(i * 256, 256), 256), :] = jnp.zeros((256, 128), jnp.float32)
        return carry

    lax.fori_loop(0, 32768 // 256, clear, 0)
    lane = lax.broadcasted_iota(jnp.int32, (1, 128), 1) // 16
    masks = [lane == i for i in range(8)]
    load.wait()
    pltpu.make_async_copy(cells_hbm, sized, sems.at[1]).wait()

    def batch(n, j):
        row = table[pl.ds(n * 128 + j, 1), :]
        places = [cells[n * 8 + i][j] for i in range(8)]
        return n % NACC, places, [grids[n % NACC][pl.ds(c, 1), :] + row for c in places]

    def scatter(t, carry):
        order = [(n, t * UNROLL + u) for u in range(UNROLL) for n in range(16)]
        ahead = batch(*order[0])
        for following in order[1:] + [None]:
            a, places, totals = ahead
            if following:
                ahead = batch(*following)
            for c, total, live in zip(places, totals, masks):
                pltpu.store(grids[a].at[pl.ds(c, 1), :], total, mask=live)
        return carry

    lax.fori_loop(0, 128 // UNROLL, scatter, 0)

    r, c = lax.broadcasted_iota(jnp.int32, (128, 128), 0), lax.broadcasted_iota(jnp.int32, (128, 128), 1)
    for rg in range(8):
        hit = (lax.rem(r, 16) == lax.rem(c, 16)) & (r // 16 == rg)
        picker[:, pl.ds(rg * 128, 128)] = jnp.where(hit, 1.0, 0.0).astype(jnp.bfloat16)

    def gather(t, carry):
        k2 = t // (4 // BLOCKS)
        rows = 128 * BLOCKS
        base = t * rows
        parts = []
        for rg in range(8):
            at = pl.ds(pl.multiple_of(rg * 4096 + base, rows), rows)
            parts.append(ga[at, :] + gb[at, :])
        hi, lo = split(jnp.concatenate(parts, axis=1))
        dims = (((1,), (1,)), ((), ()))
        block = lax.dot_general(picker[...], hi, dims, preferred_element_type=jnp.float32)
        block = block + lax.dot_general(picker[...], lo, dims, preferred_element_type=jnp.float32)
        block = block.reshape(8, 2, 8, rows)
        at = pl.ds(pl.multiple_of(lax.rem(t, 4 // BLOCKS) * rows, rows), rows)
        for v in range(2):
            for h in range(2):
                out[h, v, pl.ds(k2 * 4, 4), :, at] = block[h * 4 : h * 4 + 4, v]
        return carry

    lax.fori_loop(0, 32 // BLOCKS, gather, 0)
    body = pl.ds(0, 32)
    write = pltpu.make_async_copy(out.at[:, :, body], out_hbm.at[:, :, body], sems.at[2])
    write.start()

    quarter = lax.broadcasted_iota(jnp.int32, (32, 128), 1) // 32
    for h in range(2):
        for v in range(2):
            for side, (col, at) in enumerate(((0, 0), (384, 96))):
                for kk in range(2):
                    total = None
                    for kq in range(4):
                        x = out[h, v, pl.ds((kk * 4 + kq) * 4, 4), :, pl.ds(col, 128)].reshape(32, 128)
                        shift = (kq * 32 - at) % 128
                        x = pltpu.roll(x, shift, 1) if shift else x
                        total = x if total is None else jnp.where(quarter == kq, x, total)
                    out[h, v, pl.ds(32, 4), :, pl.ds((side * 2 + kk) * 128, 128)] = total.reshape(4, 8, 128)
    edge = pl.ds(32, 4)
    write_edge = pltpu.make_async_copy(out.at[:, :, edge], out_hbm.at[:, :, edge], sems.at[3])
    write_edge.start()
    write.wait()
    write_edge.wait()


def grid_tile(table, cells):
    hbm = pl.BlockSpec(memory_space=pl.ANY)
    return pl.pallas_call(
        grid_kernel,
        out_shape=jax.ShapeDtypeStruct((2, 2, 36, 8, 512), jnp.float32),
        in_specs=[hbm, hbm],
        out_specs=hbm,
        scratch_shapes=[
            pltpu.VMEM((2048, 128), jnp.float32),
            pltpu.VMEM((2, 2, 36, 8, 512), jnp.float32),
            pltpu.VMEM((128, 1024), jnp.bfloat16),
            pltpu.VMEM((128, 1, 128), jnp.int32),
            pltpu.SemaphoreType.DMA((4,)),
        ]
        + [pltpu.VMEM((32768, 128), jnp.float32)] * NACC
        + [pltpu.SMEM((128,), jnp.int32)] * 128,
        compiler_params=pltpu.CompilerParams(vmem_limit_bytes=VMEM),
        cost_estimate=pl.CostEstimate(flops=10**9, bytes_accessed=4 * 2**20, transcendentals=0),
        name="scatter",
    )(table, cells)


def filter_kernel(n_lat, n_lon, x_hbm, t_hbm, w_hbm, a_hbm, out, x, e, y, t, w, a, send, recv, local):
    lat = lax.axis_index("lat")
    lon = lax.axis_index("lon")
    west = lax.rem(lon + n_lon - 1, n_lon)
    east = lax.rem(lon + 1, n_lon)
    north = lat - 1
    south = lat + 1
    has_north = lat > 0
    has_south = lat < n_lat - 1
    rows = pl.ds(0, 256)
    edge = pl.ds(256, 32)
    own = pl.ds(0, 2)
    upper, lower = pl.ds(0, 248), pl.ds(8, 248)

    barrier = pltpu.get_barrier_semaphore()

    def greet(where):
        pl.semaphore_signal(barrier, inc=1, device_id=where, device_id_type=MESH)

    @pl.when(has_north)
    def _():
        greet((north, lon))

    @pl.when(has_south)
    def _():
        greet((south, lon))

    greet((lat, west))
    greet((lat, east))

    loads = [
        pltpu.make_async_copy(x_hbm.at[:, :, rows], x.at[own], local.at[0]),
        pltpu.make_async_copy(t_hbm, t, local.at[1]),
        pltpu.make_async_copy(w_hbm, w, local.at[2]),
        pltpu.make_async_copy(a_hbm, a, local.at[3]),
    ]
    for copy in loads:
        copy.start()
    ends = lat * (n_lat - 1 - lat)
    pl.semaphore_wait(barrier, jnp.where(ends == 0, 3, 4))

    def remote(src, dst, slot, where):
        return pltpu.make_async_remote_copy(
            src_ref=src, dst_ref=dst, send_sem=send.at[slot], recv_sem=recv.at[slot],
            device_id=where, device_id_type=MESH,
        )

    sides = [
        remote(x_hbm.at[:, :, edge, pl.ds(0, 256)], e.at[1, own], 0, (lat, west)),
        remote(x_hbm.at[:, :, edge, pl.ds(256, 256)], e.at[0, own], 1, (lat, east)),
    ]
    up = [
        remote(x_hbm.at[0, 0, upper], x.at[3, 0, upper], 2, (north, lon)),
        remote(x_hbm.at[0, 1, upper], x.at[3, 1, upper], 3, (north, lon)),
        remote(e.at[:, 0], e.at[:, 3], 4, (north, lon)),
    ]
    down = [
        remote(x_hbm.at[1, 0, lower], x.at[2, 0, lower], 5, (south, lon)),
        remote(x_hbm.at[1, 1, lower], x.at[2, 1, lower], 6, (south, lon)),
        remote(e.at[:, 1], e.at[:, 2], 7, (south, lon)),
    ]

    def ends_do(act, which):
        @pl.when(has_north)
        def _():
            for i in which:
                act(up[i])

        @pl.when(has_south)
        def _():
            for i in which:
                act(down[i])

    def arrived(which):
        @pl.when(has_north)
        def _():
            for i in which:
                down[i].wait_recv()

        @pl.when(has_south)
        def _():
            for i in which:
                up[i].wait_recv()

    for copy in sides:
        copy.start()
    ends_do(lambda copy: copy.start(), (0,))

    x[2, :, pl.ds(0, 8)] = jnp.zeros((2, 8, 512), jnp.float32)
    x[3, :, pl.ds(248, 8)] = jnp.zeros((2, 8, 512), jnp.float32)
    for s, there in ((2, has_north), (3, has_south)):
        @pl.when(jnp.logical_not(there))
        def _():
            x[s] = jnp.zeros((2, 256, 512), jnp.float32)
            e[:, s] = jnp.zeros((2, 2, 32, 256), jnp.float32)

    def centre(s, v):
        total = dot3(split(x[pl.ds(s, 2), v].reshape(512, 512)), (t[0, v], t[1, v]))
        for u in range(2):
            for cb in range(4):
                y[s + u, v, cb] = total[u * 256 : u * 256 + 256, cb * 128 : cb * 128 + 128]

    def rims(s, v):
        for side in range(2):
            lines = [e[side, s + u, v, :, pl.ds(kk * 128, 128)] for u in range(2) for kk in range(2)]
            rim = dot3(split(jnp.concatenate(lines, axis=0)), (w[0, v, side], w[1, v, side]))
            for u in range(2):
                for k2 in range(8):
                    line = (u * 2 + k2 // 4) * 32
                    col = (k2 % 4) * 128
                    y[s + u, v, side * 3, pl.ds(k2 * 32, 32)] += rim[line : line + 32, col : col + 128]

    def along_lat(s, v):
        def levels(i, carry):
            for u in range(4):
                l = i * 4 + u
                line = jnp.concatenate(
                    [
                        jnp.concatenate([y[s + k, v, cb, pl.ds(l, 32, stride=8), :] for cb in range(4)], axis=1)
                        for k in range(2)
                    ],
                    axis=0,
                )
                hi, lo = split(line)
                part = dot(a[s // 2, v], jnp.concatenate([hi, hi, lo], axis=0))
                out[v, l] = part if s == 0 else out[v, l] + part
            return carry

        lax.fori_loop(0, LEV // 4, levels, 0)

    for copy in loads:
        copy.wait()
    centre(0, 0)
    for copy in sides:
        copy.wait_recv()
    ends_do(lambda copy: copy.start(), (2, 1))
    centre(0, 1)
    for v in range(2):
        rims(0, v)
        along_lat(0, v)

    for v in range(2):
        arrived((v, 2) if v == 0 else (v,))
        centre(2, v)
        rims(2, v)
        along_lat(2, v)

    for copy in sides:
        copy.wait_send()
    ends_do(lambda copy: copy.wait_send(), (0, 1, 2))


def filter_tile(n_lat, n_lon, x, weights):
    return pl.pallas_call(
        functools.partial(filter_kernel, n_lat, n_lon),
        out_shape=jax.ShapeDtypeStruct((2, 8, 64, 512), jnp.float32),
        in_specs=[pl.BlockSpec(memory_space=pltpu.HBM)] * 4,
        out_specs=pl.BlockSpec(memory_space=pltpu.VMEM),
        scratch_shapes=[
            pltpu.VMEM((4, 2, 256, 512), jnp.float32),
            pltpu.VMEM((2, 4, 2, 32, 256), jnp.float32),
            pltpu.VMEM((4, 2, 4, 256, 128), jnp.float32),
            pltpu.VMEM((2, 2, 512, 512), jnp.bfloat16),
            pltpu.VMEM((2, 2, 2, 128, 512), jnp.bfloat16),
            pltpu.VMEM((2, 2, 64, 192), jnp.bfloat16),
            pltpu.SemaphoreType.DMA((8,)),
            pltpu.SemaphoreType.DMA((8,)),
            pltpu.SemaphoreType.DMA((4,)),
        ],
        compiler_params=pltpu.CompilerParams(
            vmem_limit_bytes=40 * 2**20, collective_id=0, has_side_effects=True
        ),
        cost_estimate=pl.CostEstimate(flops=6 * 10**9, bytes_accessed=8 * 2**20, transcendentals=0),
        name="filters",
    )(x, *weights)


def route_kernel(n_lat, n_lon, obs_hbm, cells_hbm, counts_hbm, lengths_hbm, weights_hbm, mix_hbm,
                 table, cells_out, t_out, w_out, a_out,
                 box, cell_box, vals, cells, counts, lengths, weights, mix, tiles, local, send, recv):
    lat = lax.axis_index("lat")
    lon = lax.axis_index("lon")
    me = lat * n_lon + lon
    count = n_lat * n_lon

    loads = [
        pltpu.make_async_copy(src, dst, local.at[i])
        for i, (src, dst) in enumerate(
            ((obs_hbm, box), (cells_hbm, cell_box), (counts_hbm, counts), (lengths_hbm, lengths),
             (weights_hbm, weights), (mix_hbm, mix))
        )
    ]
    for copy in loads:
        copy.start()

    barrier = pltpu.get_barrier_semaphore()

    def peer(k):
        return lax.rem(lat + k // n_lon, n_lat), lax.rem(lon + lax.rem(k, n_lon), n_lon)

    def greet(k, carry):
        pl.semaphore_signal(barrier, inc=1, device_id=peer(k), device_id_type=MESH)
        return carry

    lax.fori_loop(1, count, greet, 0)
    for copy in loads:
        copy.wait()

    slot = lax.broadcasted_iota(jnp.int32, (16, 128), 1)

    def mask(i, carry):
        for u in range(8):
            d = i * 8 + u
            box[d] = jnp.where(slot < counts[0, d], box[d], 0.0)
        return carry

    lax.fori_loop(0, count // 8, mask, 0)
    pl.semaphore_wait(barrier, count - 1)

    def to(k, carry):
        to_lat, to_lon = peer(k)
        d = to_lat * n_lon + to_lon
        pltpu.make_async_remote_copy(
            src_ref=cell_box.at[d], dst_ref=cells.at[me], send_sem=send.at[0], recv_sem=recv.at[n_lat],
            device_id=(to_lat, to_lon), device_id_type=MESH,
        ).start()
        pltpu.make_async_remote_copy(
            src_ref=box.at[d], dst_ref=vals.at[me], send_sem=send.at[1], recv_sem=recv.at[lat],
            device_id=(to_lat, to_lon), device_id_type=MESH,
        ).start()
        return carry

    lax.fori_loop(1, count, to, 0)
    pltpu.make_async_copy(cell_box.at[me], cells.at[me], recv.at[n_lat]).start()
    pltpu.make_async_copy(box.at[me], vals.at[me], recv.at[lat]).start()

    def iota(shape, dim):
        return lax.broadcasted_iota(jnp.int32, shape, dim)

    def profile(v, offset):
        t = offset.astype(jnp.float32)
        total = 0.0
        for s in range(3):
            scale = t / lengths[v, s]
            total = total + weights[v, s] * jnp.exp(-0.5 * (scale * scale))
        return jnp.where(jnp.abs(offset) <= HALF, total, 0.0)

    flat = (128, 128)
    for v in range(2):
        taps = profile(v, iota((8, 128), 1) - HALF)
        norm = lax.rsqrt(jnp.sum(taps * taps, axis=1, keepdims=True))[0:1, 0:1]
        for i in range(3):
            hi, lo = split(profile(v, iota(flat, 0) - iota(flat, 1) + (i - 1) * 128) * norm)
            tiles[0, i] = hi
            tiles[1, i] = lo
        blank = jnp.zeros(flat, jnp.bfloat16)
        for p in range(2):
            for i in range(4):
                for j in range(4):
                    piece = tiles[p, i - j + 1] if abs(i - j) <= 1 else blank
                    t_out[p, v, pl.ds(i * 128, 128), pl.ds(j * 128, 128)] = piece
            w_out[p, v] = jnp.zeros((2, 128, 512), jnp.bfloat16)
            for kq in range(4):
                at = pl.ds(kq * 32, 32), pl.ds(kq * 128, 128)
                w_out[(p, v, 0) + at] = tiles[p, 0, pl.ds(96, 32)]
                w_out[(p, v, 1) + at] = tiles[p, 2, pl.ds(0, 32)]
        k = iota((64, 192), 1)
        place = lax.rem(k, 32)
        inner = lax.rem(place, 4) * 8 + place // 4
        second = lax.rem(k, 64) // 32
        for part in range(2):
            base = second * 32 if part == 0 else second * 96 - 32
            hi, lo = split(profile(v, base + inner - iota((64, 192), 0)) * norm)
            a_out[part, v] = jnp.where(k // 64 == 1, lo.astype(jnp.float32), hi.astype(jnp.float32)).astype(jnp.bfloat16)

    row, col = iota((16, 128), 0), iota((16, 128), 1)
    small = jnp.zeros((16, 128), jnp.float32)
    for v in range(2):
        for l in range(LEV):
            for m in range(LEV):
                here = (row == v * LEV + m) & (lax.rem(col, 16) == v * LEV + l)
                small = jnp.where(here, mix[v, l, m], small)
    mixer = split(jnp.concatenate([jnp.where(col // 16 == i, small, 0.0) for i in range(8)], axis=0))

    def group(i, carry):
        g = lax.rem(lat + n_lat - i, n_lat)
        here = pl.ds(pl.multiple_of(g * 8, 8), 8)
        pltpu.make_async_copy(vals.at[here], vals.at[here], recv.at[g]).wait()
        rows = vals[here].reshape(128, 128).T
        table[pl.ds(pl.multiple_of(g * 128, 128), 128), :] = dot3(split(rows), mixer)
        return carry

    lax.fori_loop(0, n_lat, group, 0)
    pltpu.make_async_copy(cells, cells, recv.at[n_lat]).wait()
    cells_out[...] = cells[...]
    rest = pl.ds(0, count - 1)
    pltpu.make_async_copy(cell_box.at[rest], cells.at[rest], send.at[0]).wait()
    pltpu.make_async_copy(box.at[rest], vals.at[rest], send.at[1]).wait()


def route(n_lat, n_lon, obs, cells, counts, lengths, weights, mix):
    n = n_lat * n_lon
    hbm = pl.BlockSpec(memory_space=pl.ANY)
    bf16 = jnp.bfloat16
    return pl.pallas_call(
        functools.partial(route_kernel, n_lat, n_lon),
        out_shape=(
            jax.ShapeDtypeStruct((n * 16, 128), jnp.float32),
            jax.ShapeDtypeStruct((n, 1, 128), jnp.int32),
            jax.ShapeDtypeStruct((2, 2, 512, 512), bf16),
            jax.ShapeDtypeStruct((2, 2, 2, 128, 512), bf16),
            jax.ShapeDtypeStruct((2, 2, 64, 192), bf16),
        ),
        in_specs=[hbm] * 6,
        out_specs=[pl.BlockSpec(memory_space=pltpu.VMEM)] * 5,
        scratch_shapes=[
            pltpu.VMEM((n, 16, 128), jnp.float32),
            pltpu.VMEM((n, 1, 128), jnp.int32),
            pltpu.VMEM((n, 16, 128), jnp.float32),
            pltpu.VMEM((n, 1, 128), jnp.int32),
            pltpu.SMEM((1, n), jnp.int32),
            pltpu.SMEM((2, 3), jnp.float32),
            pltpu.SMEM((2, 3), jnp.float32),
            pltpu.SMEM((2, LEV, LEV), jnp.float32),
            pltpu.VMEM((2, 3, 128, 128), bf16),
            pltpu.SemaphoreType.DMA((6,)),
            pltpu.SemaphoreType.DMA((2,)),
            pltpu.SemaphoreType.DMA((n_lat + 1,)),
        ],
        compiler_params=pltpu.CompilerParams(vmem_limit_bytes=VMEM, collective_id=1, has_side_effects=True),
        cost_estimate=pl.CostEstimate(flops=10**7, bytes_accessed=4 * 2**20, transcendentals=0),
        name="route",
    )(obs, cells, counts, lengths, weights, mix)


def local(obs_values, obs_cells, obs_counts, filter_lengths, filter_weights, vertical_mix):
    n_lat, n_lon = lax.axis_size("lat"), lax.axis_size("lon")
    n = n_lat * n_lon
    table, cells, *weights = route(
        n_lat, n_lon, obs_values.reshape(n, 16, 128), obs_cells.reshape(n, 1, 128), obs_counts,
        filter_lengths, filter_weights, vertical_mix,
    )
    x = grid_tile(table, cells)
    return filter_tile(n_lat, n_lon, x.reshape(2, 2, 288, 512), weights)


def solution(mesh):
    in_specs = (
        P(("lat", "lon"), None, None, None, None),
        P(("lat", "lon"), None, None),
        P(("lat", "lon"), None),
        P(),
        P(),
        P(),
    )
    return jax.shard_map(
        local, mesh=mesh, in_specs=in_specs, out_specs=P(None, None, "lat", "lon"), check_vma=False
    )
```

time: 85.7 us -> 79.2 us (0.924)
  Pallas kernels: 82.4 us -> 74.3 us
  local copies, waits for them, and re-layouts: 3.14 us -> 4.58 us
    pallas_call x1, Pallas kernels: 29 us -> 23.5 us  [filter_tile(): pl.pallas_call(functools.partial(filter_kernel, n_lat, n_lon), out_shape=...]
    pallas_call x1, Pallas kernels: 25.3 us -> 22.7 us  [grid_tile(): pl.pallas_call(grid_kernel, out_shape=jax.ShapeDtypeStruct((2, 2, 36, 8,...]
    unnamed x1 -> x9, local copies, waits for them, and re-layouts: 3.14 us -> 4.58 us
where the time goes in v4:
time: 79.2 us; the launch traced here: 79 us
  Pallas kernels  74.3 us (94%)
  local copies, waits for them, and re-layouts  4.58 us (6%)
    pallas_call x1, Pallas kernels, route(): pl.pallas_call(functools.partial(route_kernel, n_lat, n_lon), out_shape=(...  28.1 us
    pallas_call x1, Pallas kernels, filter_tile(): pl.pallas_call(functools.partial(filter_kernel, n_lat, n_lon), out_shape=...  23.5 us
    pallas_call x1, Pallas kernels, grid_tile(): pl.pallas_call(grid_kernel, out_shape=jax.ShapeDtypeStruct((2, 2, 36, 8,...  22.7 us
    unnamed x9, local copies, waits for them, and re-layouts  4.58 us

profile of v4, /device:TPU:32, one launch (start us, length us, event | category | flops | bytes accessed | tf_op | source)
XLA Modules:
  0.0 79.0 jit_solution(8004645787594567388)
XLA Ops:
  0.0 28.1 %route.1 = (f32[2048,128]{1,0:T(8,128)}, s32[128,1,128]{2,1,0:T(1,128)}, bf16[2,2,512,512]{3,2,1,0:T(8,128)(2,1)}, bf16[2,2,2,128,512]{4,3,2,1,0:T(8,128)(2,1)}, bf16[2,2,64,192]{3,2,1,0:T(8,128)(2,1)}) custom-call(f32[128,16,128]{2,1,0:T(8,128)} %bitcast.4, s32[128,1,128]{2,1,0:T(1,128)} %bitcast.5, s32[1,128]{1,0:T(1,128)} %counts_hbm.1, ...), custom_call_target="tpu_custom_call" | custom-call | flops 10000000 | bytes 4194304 | tf_op jit(solution)/shard_map/route/pallas_call | solution.py:442
  28.1 0.0 copy-start.1
  28.1 0.0 copy-start.2
  28.1 22.7 %scatter.1 = f32[2,2,36,8,512]{4,3,2,1,0:T(8,128)} custom-call(f32[2048,128]{1,0:T(8,128)} %get-tuple-element.10.table_hbm, s32[128,1,128]{2,1,0:T(1,128)} %get-tuple-element.11.cells_hbm), custom_call_target="tpu_custom_call" | custom-call | flops 1000000000 | bytes 4194304 | tf_op jit(solution)/shard_map/scatter/pallas_call | solution.py:118
  50.8 0.0 copy-done.1
  50.9 0.0 copy-done.2
  50.9 0.0 copy-start
  50.9 1.6 %copy-done = bf16[2,2,512,512]{3,2,1,0:T(8,128)(2,1)S(1)} copy-done((bf16[2,2,512,512]{3,2,1,0:T(8,128)(2,1)S(1)}, bf16[2,2,512,512]{3,2,1,0:T(8,128)(2,1)}, u32[]{:S(2)}) %copy-start) | copy-done | bytes 2097176
  52.5 0.0 copy-start.3
  52.5 1.7 %copy-done.3 = f32[2,2,36,8,512]{4,3,2,1,0:T(8,128)S(1)} copy-done((f32[2,2,36,8,512]{4,3,2,1,0:T(8,128)S(1)}, f32[2,2,36,8,512]{4,3,2,1,0:T(8,128)}, u32[]{:S(2)}) %copy-start.3) | copy-done | bytes 2359320
  54.1 23.5 %filters.1 = f32[2,8,64,512]{3,2,1,0:T(8,128)S(1)} custom-call(f32[2,2,288,512]{3,2,1,0:T(8,128)S(1)} %bitcast.3, bf16[2,2,512,512]{3,2,1,0:T(8,128)(2,1)S(1)} %copy-done, bf16[2,2,2,128,512]{4,3,2,1,0:T(8,128)(2,1)S(1)} %copy-done.1, bf16[2,2,64,192]{3,2,1,0:T(8,128)(2,1)S(1)} %copy-done.2), custom_call_target="tpu_custom_call" | custom-call | flops 6000000000 | bytes 8388608 | tf_op jit(solution)/shard_map/filters/pallas_call | solution.py:291
  77.7 1.3 %copy.8 = f32[2,8,64,512]{3,2,1,0:T(8,128)} copy(f32[2,8,64,512]{3,2,1,0:T(8,128)S(1)} %filters.1) | data formatting | bytes 4194304
Async XLA Ops:
  28.1 22.7 %copy-start.1 = (bf16[2,2,2,128,512]{4,3,2,1,0:T(8,128)(2,1)S(1)}, bf16[2,2,2,128,512]{4,3,2,1,0:T(8,128)(2,1)}, u32[]{:S(2)}) copy-start(bf16[2,2,2,128,512]{4,3,2,1,0:T(8,128)(2,1)} %get-tuple-element.13.w_hbm) | copy-start | bytes 3145732
  28.1 22.7 %copy-start.2 = (bf16[2,2,64,192]{3,2,1,0:T(8,128)(2,1)S(1)}, bf16[2,2,64,192]{3,2,1,0:T(8,128)(2,1)}, u32[]{:S(2)}) copy-start(bf16[2,2,64,192]{3,2,1,0:T(8,128)(2,1)} %get-tuple-element.14.a_hbm) | copy-start | bytes 294916
  50.9 1.6 %copy-start = (bf16[2,2,512,512]{3,2,1,0:T(8,128)(2,1)S(1)}, bf16[2,2,512,512]{3,2,1,0:T(8,128)(2,1)}, u32[]{:S(2)}) copy-start(bf16[2,2,512,512]{3,2,1,0:T(8,128)(2,1)} %get-tuple-element.12.t_hbm) | copy-start | bytes 6291460
  52.5 1.7 %copy-start.3 = (f32[2,2,36,8,512]{4,3,2,1,0:T(8,128)S(1)}, f32[2,2,36,8,512]{4,3,2,1,0:T(8,128)}, u32[]{:S(2)}) copy-start(f32[2,2,36,8,512]{4,3,2,1,0:T(8,128)} %scatter.1) | copy-start | bytes 7077892

commit v5 on v4

--- a/solution.py
+++ b/solution.py
@@ -29,22 +29,37 @@
     return dot(a[0], b[0]) + dot(a[1], b[0]) + dot(a[0], b[1])
 
 
-def grid_kernel(table_hbm, cells_hbm, out_hbm, table, out, picker, sized, sems, ga, gb, *cells):
+def grid_kernel(vals_hbm, cells_hbm, mixer_hbm, out_hbm, vals, mixer, table, out, picker, sized, sems, ga, gb, *cells):
     grids = (ga, gb)
-    load = pltpu.make_async_copy(table_hbm, table, sems.at[0])
-    load.start()
+    loads = [
+        pltpu.make_async_copy(vals_hbm, vals, sems.at[0]),
+        pltpu.make_async_copy(mixer_hbm, mixer, sems.at[2]),
+    ]
+    for copy in loads:
+        copy.start()
     for s in range(128):
         pltpu.make_async_copy(cells_hbm.at[s, 0], cells[s], sems.at[1]).start()
 
     def clear(i, carry):
-        for grid in grids:
-            grid[pl.ds(pl.multiple_of(i * 256, 256), 256), :] = jnp.zeros((256, 128), jnp.float32)
+        gb[pl.ds(pl.multiple_of(i * 512, 512), 512), :] = jnp.zeros((512, 128), jnp.float32)
         return carry
 
-    lax.fori_loop(0, 32768 // 256, clear, 0)
+    lax.fori_loop(0, 64, clear, 0)
+    for copy in loads:
+        copy.wait()
+    mix = split(mixer[...])
+
+    def fill(i, carry):
+        ga[pl.ds(pl.multiple_of(i * 4096, 4096), 4096), :] = jnp.zeros((4096, 128), jnp.float32)
+        for u in range(2):
+            g = i * 2 + u
+            rows = vals[pl.ds(pl.multiple_of(g * 8, 8), 8)].reshape(128, 128).T
+            table[pl.ds(pl.multiple_of(g * 128, 128), 128), :] = dot3(split(rows), mix)
+        return carry
+
+    lax.fori_loop(0, 8, fill, 0)
     lane = lax.broadcasted_iota(jnp.int32, (1, 128), 1) // 16
     masks = [lane == i for i in range(8)]
-    load.wait()
     pltpu.make_async_copy(cells_hbm, sized, sems.at[1]).wait()
 
     def batch(n, j):
@@ -113,14 +128,16 @@
     write_edge.wait()
 
 
-def grid_tile(table, cells):
+def grid_tile(vals, cells, mixer):
     hbm = pl.BlockSpec(memory_space=pl.ANY)
     return pl.pallas_call(
         grid_kernel,
         out_shape=jax.ShapeDtypeStruct((2, 2, 36, 8, 512), jnp.float32),
-        in_specs=[hbm, hbm],
+        in_specs=[hbm] * 3,
         out_specs=hbm,
         scratch_shapes=[
+            pltpu.VMEM((128, 16, 128), jnp.float32),
+            pltpu.VMEM((128, 128), jnp.float32),
             pltpu.VMEM((2048, 128), jnp.float32),
             pltpu.VMEM((2, 2, 36, 8, 512), jnp.float32),
             pltpu.VMEM((128, 1024), jnp.bfloat16),
@@ -132,10 +149,10 @@
         compiler_params=pltpu.CompilerParams(vmem_limit_bytes=VMEM),
         cost_estimate=pl.CostEstimate(flops=10**9, bytes_accessed=4 * 2**20, transcendentals=0),
         name="scatter",
-    )(table, cells)
-
-
-def filter_kernel(n_lat, n_lon, x_hbm, t_hbm, w_hbm, a_hbm, out, x, e, y, t, w, a, send, recv, local):
+    )(vals, cells, mixer)
+
+
+def filter_kernel(n_lat, n_lon, x_hbm, t_hbm, a_hbm, out, x, e, y, t, a, send, recv, local):
     lat = lax.axis_index("lat")
     lon = lax.axis_index("lon")
     west = lax.rem(lon + n_lon - 1, n_lon)
@@ -168,8 +185,7 @@
     loads = [
         pltpu.make_async_copy(x_hbm.at[:, :, rows], x.at[own], local.at[0]),
         pltpu.make_async_copy(t_hbm, t, local.at[1]),
-        pltpu.make_async_copy(w_hbm, w, local.at[2]),
-        pltpu.make_async_copy(a_hbm, a, local.at[3]),
+        pltpu.make_async_copy(a_hbm, a, local.at[2]),
     ]
     for copy in loads:
         copy.start()
@@ -232,7 +248,7 @@
             e[:, s] = jnp.zeros((2, 2, 32, 256), jnp.float32)
 
     def centre(s, v):
-        total = dot3(split(x[pl.ds(s, 2), v].reshape(512, 512)), (t[0, v], t[1, v]))
+        total = dot3(split(x[pl.ds(s, 2), v].reshape(512, 512)), (t[0, v, 0:512], t[1, v, 0:512]))
         for u in range(2):
             for cb in range(4):
                 y[s + u, v, cb] = total[u * 256 : u * 256 + 256, cb * 128 : cb * 128 + 128]
@@ -240,7 +256,7 @@
     def rims(s, v):
         for side in range(2):
             lines = [e[side, s + u, v, :, pl.ds(kk * 128, 128)] for u in range(2) for kk in range(2)]
-            rim = dot3(split(jnp.concatenate(lines, axis=0)), (w[0, v, side], w[1, v, side]))
+            rim = dot3(split(jnp.concatenate(lines, axis=0)), (t[0, v, pl.ds(512 + side * 128, 128)], t[1, v, pl.ds(512 + side * 128, 128)]))
             for u in range(2):
                 for k2 in range(8):
                     line = (u * 2 + k2 // 4) * 32
@@ -291,21 +307,20 @@
     return pl.pallas_call(
         functools.partial(filter_kernel, n_lat, n_lon),
         out_shape=jax.ShapeDtypeStruct((2, 8, 64, 512), jnp.float32),
-        in_specs=[pl.BlockSpec(memory_space=pltpu.HBM)] * 4,
+        in_specs=[pl.BlockSpec(memory_space=pl.ANY)] * 3,
         out_specs=pl.BlockSpec(memory_space=pltpu.VMEM),
         scratch_shapes=[
             pltpu.VMEM((4, 2, 256, 512), jnp.float32),
             pltpu.VMEM((2, 4, 2, 32, 256), jnp.float32),
             pltpu.VMEM((4, 2, 4, 256, 128), jnp.float32),
-            pltpu.VMEM((2, 2, 512, 512), jnp.bfloat16),
-            pltpu.VMEM((2, 2, 2, 128, 512), jnp.bfloat16),
+            pltpu.VMEM((2, 2, 768, 512), jnp.bfloat16),
             pltpu.VMEM((2, 2, 64, 192), jnp.bfloat16),
             pltpu.SemaphoreType.DMA((8,)),
             pltpu.SemaphoreType.DMA((8,)),
-            pltpu.SemaphoreType.DMA((4,)),
+            pltpu.SemaphoreType.DMA((3,)),
         ],
         compiler_params=pltpu.CompilerParams(
-            vmem_limit_bytes=40 * 2**20, collective_id=0, has_side_effects=True
+            vmem_limit_bytes=101 * 2**19, collective_id=0, has_side_effects=True
         ),
         cost_estimate=pl.CostEstimate(flops=6 * 10**9, bytes_accessed=8 * 2**20, transcendentals=0),
         name="filters",
@@ -313,8 +328,8 @@
 
 
 def route_kernel(n_lat, n_lon, obs_hbm, cells_hbm, counts_hbm, lengths_hbm, weights_hbm, mix_hbm,
-                 table, cells_out, t_out, w_out, a_out,
-                 box, cell_box, vals, cells, counts, lengths, weights, mix, tiles, local, send, recv):
+                 vals, cells, mixer, t_out, a_out,
+                 box, cell_box, counts, lengths, weights, mix, tiles, local, send, recv):
     lat = lax.axis_index("lat")
     lon = lax.axis_index("lon")
     me = lat * n_lon + lon
@@ -332,14 +347,23 @@
 
     barrier = pltpu.get_barrier_semaphore()
 
-    def peer(k):
-        return lax.rem(lat + k // n_lon, n_lat), lax.rem(lon + lax.rem(k, n_lon), n_lon)
-
-    def greet(k, carry):
-        pl.semaphore_signal(barrier, inc=1, device_id=peer(k), device_id_type=MESH)
-        return carry
-
-    lax.fori_loop(1, count, greet, 0)
+    columns = [lon] + [lax.rem(lon + k, n_lon) for k in range(1, n_lon)]
+
+    def each_peer(act):
+        for k in range(1, n_lon):
+            act(lat, columns[k])
+
+        def line(i, carry):
+            for column in columns:
+                act(lax.rem(lat + i, n_lat), column)
+            return carry
+
+        lax.fori_loop(1, n_lat, line, 0)
+
+    def greet(to_lat, to_lon):
+        pl.semaphore_signal(barrier, inc=1, device_id=(to_lat, to_lon), device_id_type=MESH)
+
+    each_peer(greet)
     for copy in loads:
         copy.wait()
 
@@ -354,22 +378,17 @@
     lax.fori_loop(0, count // 8, mask, 0)
     pl.semaphore_wait(barrier, count - 1)
 
-    def to(k, carry):
-        to_lat, to_lon = peer(k)
+    def give(to_lat, to_lon):
         d = to_lat * n_lon + to_lon
-        pltpu.make_async_remote_copy(
-            src_ref=cell_box.at[d], dst_ref=cells.at[me], send_sem=send.at[0], recv_sem=recv.at[n_lat],
-            device_id=(to_lat, to_lon), device_id_type=MESH,
-        ).start()
-        pltpu.make_async_remote_copy(
-            src_ref=box.at[d], dst_ref=vals.at[me], send_sem=send.at[1], recv_sem=recv.at[lat],
-            device_id=(to_lat, to_lon), device_id_type=MESH,
-        ).start()
-        return carry
-
-    lax.fori_loop(1, count, to, 0)
-    pltpu.make_async_copy(cell_box.at[me], cells.at[me], recv.at[n_lat]).start()
-    pltpu.make_async_copy(box.at[me], vals.at[me], recv.at[lat]).start()
+        for i, (src, dst) in enumerate(((box, vals), (cell_box, cells))):
+            pltpu.make_async_remote_copy(
+                src_ref=src.at[d], dst_ref=dst.at[me], send_sem=send.at[i], recv_sem=recv.at[i],
+                device_id=(to_lat, to_lon), device_id_type=MESH,
+            ).start()
+
+    each_peer(give)
+    pltpu.make_async_copy(cell_box.at[me], cells.at[me], recv.at[1]).start()
+    pltpu.make_async_copy(box.at[me], vals.at[me], recv.at[0]).start()
 
     def iota(shape, dim):
         return lax.broadcasted_iota(jnp.int32, shape, dim)
@@ -396,11 +415,11 @@
                 for j in range(4):
                     piece = tiles[p, i - j + 1] if abs(i - j) <= 1 else blank
                     t_out[p, v, pl.ds(i * 128, 128), pl.ds(j * 128, 128)] = piece
-            w_out[p, v] = jnp.zeros((2, 128, 512), jnp.bfloat16)
+            t_out[p, v, pl.ds(512, 256)] = jnp.zeros((256, 512), jnp.bfloat16)
             for kq in range(4):
-                at = pl.ds(kq * 32, 32), pl.ds(kq * 128, 128)
-                w_out[(p, v, 0) + at] = tiles[p, 0, pl.ds(96, 32)]
-                w_out[(p, v, 1) + at] = tiles[p, 2, pl.ds(0, 32)]
+                at = pl.ds(kq * 128, 128)
+                t_out[p, v, pl.ds(512 + kq * 32, 32), at] = tiles[p, 0, pl.ds(96, 32)]
+                t_out[p, v, pl.ds(640 + kq * 32, 32), at] = tiles[p, 2, pl.ds(0, 32)]
         k = iota((64, 192), 1)
         place = lax.rem(k, 32)
         inner = lax.rem(place, 4) * 8 + place // 4
@@ -417,22 +436,13 @@
             for m in range(LEV):
                 here = (row == v * LEV + m) & (lax.rem(col, 16) == v * LEV + l)
                 small = jnp.where(here, mix[v, l, m], small)
-    mixer = split(jnp.concatenate([jnp.where(col // 16 == i, small, 0.0) for i in range(8)], axis=0))
-
-    def group(i, carry):
-        g = lax.rem(lat + n_lat - i, n_lat)
-        here = pl.ds(pl.multiple_of(g * 8, 8), 8)
-        pltpu.make_async_copy(vals.at[here], vals.at[here], recv.at[g]).wait()
-        rows = vals[here].reshape(128, 128).T
-        table[pl.ds(pl.multiple_of(g * 128, 128), 128), :] = dot3(split(rows), mixer)
-        return carry
-
-    lax.fori_loop(0, n_lat, group, 0)
-    pltpu.make_async_copy(cells, cells, recv.at[n_lat]).wait()
-    cells_out[...] = cells[...]
+    for i in range(8):
+        mixer[pl.ds(i * 16, 16)] = jnp.where(col // 16 == i, small, 0.0)
+
     rest = pl.ds(0, count - 1)
-    pltpu.make_async_copy(cell_box.at[rest], cells.at[rest], send.at[0]).wait()
-    pltpu.make_async_copy(box.at[rest], vals.at[rest], send.at[1]).wait()
+    for i, (src, dst) in enumerate(((box, vals), (cell_box, cells))):
+        pltpu.make_async_copy(dst, dst, recv.at[i]).wait()
+        pltpu.make_async_copy(src.at[rest], dst.at[rest], send.at[i]).wait()
 
 
 def route(n_lat, n_lon, obs, cells, counts, lengths, weights, mix):
@@ -442,17 +452,15 @@
     return pl.pallas_call(
         functools.partial(route_kernel, n_lat, n_lon),
         out_shape=(
-            jax.ShapeDtypeStruct((n * 16, 128), jnp.float32),
+            jax.ShapeDtypeStruct((n, 16, 128), jnp.float32),
             jax.ShapeDtypeStruct((n, 1, 128), jnp.int32),
-            jax.ShapeDtypeStruct((2, 2, 512, 512), bf16),
-            jax.ShapeDtypeStruct((2, 2, 2, 128, 512), bf16),
+            jax.ShapeDtypeStruct((128, 128), jnp.float32),
+            jax.ShapeDtypeStruct((2, 2, 768, 512), bf16),
             jax.ShapeDtypeStruct((2, 2, 64, 192), bf16),
         ),
         in_specs=[hbm] * 6,
-        out_specs=[pl.BlockSpec(memory_space=pltpu.VMEM)] * 5,
+        out_specs=[hbm] * 2 + [pl.BlockSpec(memory_space=pltpu.VMEM)] * 3,
         scratch_shapes=[
-            pltpu.VMEM((n, 16, 128), jnp.float32),
-            pltpu.VMEM((n, 1, 128), jnp.int32),
             pltpu.VMEM((n, 16, 128), jnp.float32),
             pltpu.VMEM((n, 1, 128), jnp.int32),
             pltpu.SMEM((1, n), jnp.int32),
@@ -462,7 +470,7 @@
             pltpu.VMEM((2, 3, 128, 128), bf16),
             pltpu.SemaphoreType.DMA((6,)),
             pltpu.SemaphoreType.DMA((2,)),
-            pltpu.SemaphoreType.DMA((n_lat + 1,)),
+            pltpu.SemaphoreType.DMA((2,)),
         ],
         compiler_params=pltpu.CompilerParams(vmem_limit_bytes=VMEM, collective_id=1, has_side_effects=True),
         cost_estimate=pl.CostEstimate(flops=10**7, bytes_accessed=4 * 2**20, transcendentals=0),
@@ -473,11 +481,11 @@
 def local(obs_values, obs_cells, obs_counts, filter_lengths, filter_weights, vertical_mix):
     n_lat, n_lon = lax.axis_size("lat"), lax.axis_size("lon")
     n = n_lat * n_lon
-    table, cells, *weights = route(
+    vals, cells, mixer, *weights = route(
         n_lat, n_lon, obs_values.reshape(n, 16, 128), obs_cells.reshape(n, 1, 128), obs_counts,
         filter_lengths, filter_weights, vertical_mix,
     )
-    x = grid_tile(table, cells)
+    x = grid_tile(vals, cells, mixer)
     return filter_tile(n_lat, n_lon, x.reshape(2, 2, 288, 512), weights)
 
 

time: 79.2 us -> 75 us (0.947)
  local copies, waits for them, and re-layouts: 4.58 us -> 1.33 us
  Pallas kernels: 74.3 us -> 73.5 us
    unnamed x9 -> x3, local copies, waits for them, and re-layouts: 4.58 us -> 1.33 us
    pallas_call x1, Pallas kernels: 28.1 us -> 25.2 us  [route(): pl.pallas_call(functools.partial(route_kernel, n_lat, n_lon), out_shape=(...]
    pallas_call x1, Pallas kernels: 22.7 us -> 24.2 us  [grid_tile(): pl.pallas_call(grid_kernel, out_shape=jax.ShapeDtypeStruct((2, 2, 36, 8,...]
where the time goes in v5:
time: 75 us; the launch traced here: 74.8 us
  Pallas kernels  73.5 us (98%)
  local copies, waits for them, and re-layouts  1.33 us (2%)
    pallas_call x1, Pallas kernels, route(): pl.pallas_call(functools.partial(route_kernel, n_lat, n_lon), out_shape=(...  25.2 us
    pallas_call x1, Pallas kernels, grid_tile(): pl.pallas_call(grid_kernel, out_shape=jax.ShapeDtypeStruct((2, 2, 36, 8,...  24.2 us
    pallas_call x1, Pallas kernels, filter_tile(): pl.pallas_call(functools.partial(filter_kernel, n_lat, n_lon), out_shape=...  24.1 us

profile of v5, /device:TPU:32, one launch (start us, length us, event | category | flops | bytes accessed | tf_op | source)
XLA Modules:
  0.0 74.8 jit_solution(17976853131953042622)
XLA Ops:
  0.0 25.2 %route.1 = (f32[128,16,128]{2,1,0:T(8,128)}, s32[128,1,128]{2,1,0:T(1,128)}, f32[128,128]{1,0:T(8,128)}, bf16[2,2,768,512]{3,2,1,0:T(8,128)(2,1)}, bf16[2,2,64,192]{3,2,1,0:T(8,128)(2,1)}) custom-call(f32[128,16,128]{2,1,0:T(8,128)} %bitcast.3, s32[128,1,128]{2,1,0:T(1,128)} %bitcast.4, s32[1,128]{1,0:T(1,128)} %counts_hbm.1, f32[2,3]{1,0:T(2,128)} %lengths_hbm.1, ...), custom_call_target="tpu_custom_call" | custom-call | flops 10000000 | bytes 4194304 | tf_op jit(solution)/shard_map/route/pallas_call | solution.py:452
  25.2 0.0 copy-start
  25.2 24.2 %scatter.1 = f32[2,2,36,8,512]{4,3,2,1,0:T(8,128)} custom-call(f32[128,16,128]{2,1,0:T(8,128)} %get-tuple-element.10.vals_hbm, s32[128,1,128]{2,1,0:T(1,128)} %get-tuple-element.11.cells_hbm, f32[128,128]{1,0:T(8,128)} %get-tuple-element.12.mixer_hbm), custom_call_target="tpu_custom_call" | custom-call | flops 1000000000 | bytes 4194304 | tf_op jit(solution)/shard_map/scatter/pallas_call | solution.py:133
  49.4 0.0 copy-done
  49.4 24.1 %filters.1 = f32[2,8,64,512]{3,2,1,0:T(8,128)S(1)} custom-call(f32[2,2,288,512]{3,2,1,0:T(8,128)} %bitcast.5, bf16[2,2,768,512]{3,2,1,0:T(8,128)(2,1)} %get-tuple-element.13.t_hbm, bf16[2,2,64,192]{3,2,1,0:T(8,128)(2,1)S(1)} %copy-done), custom_call_target="tpu_custom_call" | custom-call | flops 6000000000 | bytes 8388608 | tf_op jit(solution)/shard_map/filters/pallas_call | solution.py:307
  73.5 1.3 %copy.8 = f32[2,8,64,512]{3,2,1,0:T(8,128)} copy(f32[2,8,64,512]{3,2,1,0:T(8,128)S(1)} %filters.1) | data formatting | bytes 4194304
Async XLA Ops:
  25.2 24.2 %copy-start = (bf16[2,2,64,192]{3,2,1,0:T(8,128)(2,1)S(1)}, bf16[2,2,64,192]{3,2,1,0:T(8,128)(2,1)}, u32[]{:S(2)}) copy-start(bf16[2,2,64,192]{3,2,1,0:T(8,128)(2,1)} %get-tuple-element.14.a_hbm) | copy-start | bytes 294916

commit v6 on v5

--- a/solution.py
+++ b/solution.py
@@ -9,8 +9,9 @@
 
 HALF = 31
 LEV = 8
-NACC = 2
-UNROLL = 2
+NACC = 3
+UNROLL = 4
+AHEAD = 1
 BLOCKS = 4
 VMEM = 62 * 2**20
 MESH = pl.DeviceIdType.MESH
@@ -29,8 +30,8 @@
     return dot(a[0], b[0]) + dot(a[1], b[0]) + dot(a[0], b[1])
 
 
-def grid_kernel(vals_hbm, cells_hbm, mixer_hbm, out_hbm, vals, mixer, table, out, picker, sized, sems, ga, gb, *cells):
-    grids = (ga, gb)
+def grid_kernel(vals_hbm, cells_hbm, mixer_hbm, out_hbm, vals, mixer, table, out, picker, sized, sems, ga, gb, gc, *cells):
+    grids = (ga, gb, gc)
     loads = [
         pltpu.make_async_copy(vals_hbm, vals, sems.at[0]),
         pltpu.make_async_copy(mixer_hbm, mixer, sems.at[2]),
@@ -41,7 +42,8 @@
         pltpu.make_async_copy(cells_hbm.at[s, 0], cells[s], sems.at[1]).start()
 
     def clear(i, carry):
-        gb[pl.ds(pl.multiple_of(i * 512, 512), 512), :] = jnp.zeros((512, 128), jnp.float32)
+        for grid in (gb, gc):
+            grid[pl.ds(pl.multiple_of(i * 512, 512), 512), :] = jnp.zeros((512, 128), jnp.float32)
         return carry
 
     lax.fori_loop(0, 64, clear, 0)
@@ -62,20 +64,21 @@
     masks = [lane == i for i in range(8)]
     pltpu.make_async_copy(cells_hbm, sized, sems.at[1]).wait()
 
-    def batch(n, j):
+    def batch(turn, n, j):
+        grid = grids[turn % NACC]
         row = table[pl.ds(n * 128 + j, 1), :]
         places = [cells[n * 8 + i][j] for i in range(8)]
-        return n % NACC, places, [grids[n % NACC][pl.ds(c, 1), :] + row for c in places]
+        return grid, places, [grid[pl.ds(c, 1), :] + row for c in places]
 
     def scatter(t, carry):
         order = [(n, t * UNROLL + u) for u in range(UNROLL) for n in range(16)]
-        ahead = batch(*order[0])
-        for following in order[1:] + [None]:
-            a, places, totals = ahead
-            if following:
-                ahead = batch(*following)
+        ahead = [batch(i, *order[i]) for i in range(AHEAD)]
+        for i in range(len(order)):
+            grid, places, totals = ahead.pop(0)
+            if i + AHEAD < len(order):
+                ahead.append(batch(i + AHEAD, *order[i + AHEAD]))
             for c, total, live in zip(places, totals, masks):
-                pltpu.store(grids[a].at[pl.ds(c, 1), :], total, mask=live)
+                pltpu.store(grid.at[pl.ds(c, 1), :], total, mask=live)
         return carry
 
     lax.fori_loop(0, 128 // UNROLL, scatter, 0)
@@ -92,7 +95,7 @@
         parts = []
         for rg in range(8):
             at = pl.ds(pl.multiple_of(rg * 4096 + base, rows), rows)
-            parts.append(ga[at, :] + gb[at, :])
+            parts.append(ga[at, :] + gb[at, :] + gc[at, :])
         hi, lo = split(jnp.concatenate(parts, axis=1))
         dims = (((1,), (1,)), ((), ()))
         block = lax.dot_general(picker[...], hi, dims, preferred_element_type=jnp.float32)
@@ -204,12 +207,14 @@
     ]
     up = [
         remote(x_hbm.at[0, 0, upper], x.at[3, 0, upper], 2, (north, lon)),
-        remote(x_hbm.at[0, 1, upper], x.at[3, 1, upper], 3, (north, lon)),
+        remote(x_hbm.at[0, 1, pl.ds(0, 128)], x.at[3, 1, pl.ds(0, 128)], 3, (north, lon)),
+        remote(x_hbm.at[0, 1, pl.ds(128, 120)], x.at[3, 1, pl.ds(128, 120)], 8, (north, lon)),
         remote(e.at[:, 0], e.at[:, 3], 4, (north, lon)),
     ]
     down = [
         remote(x_hbm.at[1, 0, lower], x.at[2, 0, lower], 5, (south, lon)),
-        remote(x_hbm.at[1, 1, lower], x.at[2, 1, lower], 6, (south, lon)),
+        remote(x_hbm.at[1, 1, pl.ds(128, 128)], x.at[2, 1, pl.ds(128, 128)], 6, (south, lon)),
+        remote(x_hbm.at[1, 1, pl.ds(8, 120)], x.at[2, 1, pl.ds(8, 120)], 9, (south, lon)),
         remote(e.at[:, 1], e.at[:, 2], 7, (south, lon)),
     ]
 
@@ -237,7 +242,7 @@
 
     for copy in sides:
         copy.start()
-    ends_do(lambda copy: copy.start(), (0,))
+    ends_do(lambda copy: copy.start(), (0, 1))
 
     x[2, :, pl.ds(0, 8)] = jnp.zeros((2, 8, 512), jnp.float32)
     x[3, :, pl.ds(248, 8)] = jnp.zeros((2, 8, 512), jnp.float32)
@@ -248,10 +253,14 @@
             e[:, s] = jnp.zeros((2, 2, 32, 256), jnp.float32)
 
     def centre(s, v):
-        total = dot3(split(x[pl.ds(s, 2), v].reshape(512, 512)), (t[0, v, 0:512], t[1, v, 0:512]))
-        for u in range(2):
-            for cb in range(4):
-                y[s + u, v, cb] = total[u * 256 : u * 256 + 256, cb * 128 : cb * 128 + 128]
+        hi, lo = split(x[pl.ds(s, 2), v].reshape(512, 512))
+        for n in range(2):
+            deep, wide = slice(n * 128, n * 128 + 384), pl.ds(n * 256, 256)
+            band = t[0, v, pl.ds(n * 128, 384), wide], t[1, v, pl.ds(n * 128, 384), wide]
+            total = dot3((hi[:, deep], lo[:, deep]), band)
+            for u in range(2):
+                for cb in range(2):
+                    y[s + u, v, n * 2 + cb] = total[u * 256 : u * 256 + 256, cb * 128 : cb * 128 + 128]
 
     def rims(s, v):
         for side in range(2):
@@ -286,21 +295,21 @@
     centre(0, 0)
     for copy in sides:
         copy.wait_recv()
-    ends_do(lambda copy: copy.start(), (2, 1))
+    ends_do(lambda copy: copy.start(), (3, 2))
     centre(0, 1)
     for v in range(2):
         rims(0, v)
         along_lat(0, v)
 
     for v in range(2):
-        arrived((v, 2) if v == 0 else (v,))
+        arrived((0, 3) if v == 0 else (1, 2))
         centre(2, v)
         rims(2, v)
         along_lat(2, v)
 
     for copy in sides:
         copy.wait_send()
-    ends_do(lambda copy: copy.wait_send(), (0, 1, 2))
+    ends_do(lambda copy: copy.wait_send(), (0, 1, 2, 3))
 
 
 def filter_tile(n_lat, n_lon, x, weights):
@@ -315,8 +324,8 @@
             pltpu.VMEM((4, 2, 4, 256, 128), jnp.float32),
             pltpu.VMEM((2, 2, 768, 512), jnp.bfloat16),
             pltpu.VMEM((2, 2, 64, 192), jnp.bfloat16),
-            pltpu.SemaphoreType.DMA((8,)),
-            pltpu.SemaphoreType.DMA((8,)),
+            pltpu.SemaphoreType.DMA((10,)),
+            pltpu.SemaphoreType.DMA((10,)),
             pltpu.SemaphoreType.DMA((3,)),
         ],
         compiler_params=pltpu.CompilerParams(

time: 75 us -> 74 us (0.987)
  Pallas kernels: 73.5 us -> 72.5 us
    pallas_call x1, Pallas kernels: 24.2 us -> 23.1 us  [grid_tile(): pl.pallas_call(grid_kernel, out_shape=jax.ShapeDtypeStruct((2, 2, 36, 8,...]
where the time goes in v6:
time: 74 us; the launch traced here: 73.9 us
  Pallas kernels  72.5 us (98%)
  local copies, waits for them, and re-layouts  1.33 us (2%)
    pallas_call x1, Pallas kernels, route(): pl.pallas_call(functools.partial(route_kernel, n_lat, n_lon), out_shape=(...  25.2 us
    pallas_call x1, Pallas kernels, filter_tile(): pl.pallas_call(functools.partial(filter_kernel, n_lat, n_lon), out_shape=...  24.1 us
    pallas_call x1, Pallas kernels, grid_tile(): pl.pallas_call(grid_kernel, out_shape=jax.ShapeDtypeStruct((2, 2, 36, 8,...  23.1 us

profile of v6, /device:TPU:32, one launch (start us, length us, event | category | flops | bytes accessed | tf_op | source)
XLA Modules:
  0.0 73.9 jit_solution(1866014844190300587)
XLA Ops:
  0.0 25.2 %route.1 = (f32[128,16,128]{2,1,0:T(8,128)}, s32[128,1,128]{2,1,0:T(1,128)}, f32[128,128]{1,0:T(8,128)}, bf16[2,2,768,512]{3,2,1,0:T(8,128)(2,1)}, bf16[2,2,64,192]{3,2,1,0:T(8,128)(2,1)}) custom-call(f32[128,16,128]{2,1,0:T(8,128)} %bitcast.3, s32[128,1,128]{2,1,0:T(1,128)} %bitcast.4, s32[1,128]{1,0:T(1,128)} %counts_hbm.1, f32[2,3]{1,0:T(2,128)} %lengths_hbm.1, ...), custom_call_target="tpu_custom_call" | custom-call | flops 10000000 | bytes 4194304 | tf_op jit(solution)/shard_map/route/pallas_call | solution.py:461
  25.2 0.0 copy-start
  25.2 23.1 %scatter.1 = f32[2,2,36,8,512]{4,3,2,1,0:T(8,128)} custom-call(f32[128,16,128]{2,1,0:T(8,128)} %get-tuple-element.10.vals_hbm, s32[128,1,128]{2,1,0:T(1,128)} %get-tuple-element.11.cells_hbm, f32[128,128]{1,0:T(8,128)} %get-tuple-element.12.mixer_hbm), custom_call_target="tpu_custom_call" | custom-call | flops 1000000000 | bytes 4194304 | tf_op jit(solution)/shard_map/scatter/pallas_call | solution.py:136
  48.4 0.0 copy-done
  48.4 24.1 %filters.1 = f32[2,8,64,512]{3,2,1,0:T(8,128)S(1)} custom-call(f32[2,2,288,512]{3,2,1,0:T(8,128)} %bitcast.5, bf16[2,2,768,512]{3,2,1,0:T(8,128)(2,1)} %get-tuple-element.13.t_hbm, bf16[2,2,64,192]{3,2,1,0:T(8,128)(2,1)S(1)} %copy-done), custom_call_target="tpu_custom_call" | custom-call | flops 6000000000 | bytes 8388608 | tf_op jit(solution)/shard_map/filters/pallas_call | solution.py:316
  72.5 1.3 %copy.8 = f32[2,8,64,512]{3,2,1,0:T(8,128)} copy(f32[2,8,64,512]{3,2,1,0:T(8,128)S(1)} %filters.1) | data formatting | bytes 4194304
Async XLA Ops:
  25.2 23.2 %copy-start = (bf16[2,2,64,192]{3,2,1,0:T(8,128)(2,1)S(1)}, bf16[2,2,64,192]{3,2,1,0:T(8,128)(2,1)}, u32[]{:S(2)}) copy-start(bf16[2,2,64,192]{3,2,1,0:T(8,128)(2,1)} %get-tuple-element.14.a_hbm) | copy-start | bytes 294916

commit v7 on v6

--- a/solution.py
+++ b/solution.py
@@ -30,7 +30,7 @@
     return dot(a[0], b[0]) + dot(a[1], b[0]) + dot(a[0], b[1])
 
 
-def grid_kernel(vals_hbm, cells_hbm, mixer_hbm, out_hbm, vals, mixer, table, out, picker, sized, sems, ga, gb, gc, *cells):
+def grid_kernel(vals_hbm, cells_hbm, mixer_hbm, out_hbm, vals, mixer, table, out, picker, sized, sems, stores, ga, gb, gc, *cells):
     grids = (ga, gb, gc)
     loads = [
         pltpu.make_async_copy(vals_hbm, vals, sems.at[0]),
@@ -88,8 +88,12 @@
         hit = (lax.rem(r, 16) == lax.rem(c, 16)) & (r // 16 == rg)
         picker[:, pl.ds(rg * 128, 128)] = jnp.where(hit, 1.0, 0.0).astype(jnp.bfloat16)
 
-    def gather(t, carry):
-        k2 = t // (4 // BLOCKS)
+    def write(k2):
+        at = pl.ds(k2 * 4, 4)
+        return pltpu.make_async_copy(out.at[:, :, at], out_hbm.at[:, :, at], stores.at[k2])
+
+    def gather(k2, carry):
+        t = k2
         rows = 128 * BLOCKS
         base = t * rows
         parts = []
@@ -105,12 +109,10 @@
         for v in range(2):
             for h in range(2):
                 out[h, v, pl.ds(k2 * 4, 4), :, at] = block[h * 4 : h * 4 + 4, v]
+        write(k2).start()
         return carry
 
-    lax.fori_loop(0, 32 // BLOCKS, gather, 0)
-    body = pl.ds(0, 32)
-    write = pltpu.make_async_copy(out.at[:, :, body], out_hbm.at[:, :, body], sems.at[2])
-    write.start()
+    lax.fori_loop(0, 8, gather, 0)
 
     quarter = lax.broadcasted_iota(jnp.int32, (32, 128), 1) // 32
     for h in range(2):
@@ -127,7 +129,8 @@
     edge = pl.ds(32, 4)
     write_edge = pltpu.make_async_copy(out.at[:, :, edge], out_hbm.at[:, :, edge], sems.at[3])
     write_edge.start()
-    write.wait()
+    for k2 in range(8):
+        write(k2).wait()
     write_edge.wait()
 
 
@@ -146,6 +149,7 @@
             pltpu.VMEM((128, 1024), jnp.bfloat16),
             pltpu.VMEM((128, 1, 128), jnp.int32),
             pltpu.SemaphoreType.DMA((4,)),
+            pltpu.SemaphoreType.DMA((8,)),
         ]
         + [pltpu.VMEM((32768, 128), jnp.float32)] * NACC
         + [pltpu.SMEM((128,), jnp.int32)] * 128,
@@ -155,7 +159,7 @@
     )(vals, cells, mixer)
 
 
-def filter_kernel(n_lat, n_lon, x_hbm, t_hbm, a_hbm, out, x, e, y, t, a, send, recv, local):
+def filter_kernel(n_lat, n_lon, x_hbm, t_hbm, a_hbm, out, x, e, y, t, a, passing, send, recv, local):
     lat = lax.axis_index("lat")
     lon = lax.axis_index("lon")
     west = lax.rem(lon + n_lon - 1, n_lon)
@@ -164,6 +168,9 @@
     south = lat + 1
     has_north = lat > 0
     has_south = lat < n_lat - 1
+    last, mid = n_lat - 1, n_lat // 2 - 1
+    at_end = (lat == 0) | (lat == last)
+    at_mid = (lat == mid) | (lat == mid + 1)
     rows = pl.ds(0, 256)
     edge = pl.ds(256, 32)
     own = pl.ds(0, 2)
@@ -185,6 +192,16 @@
     greet((lat, west))
     greet((lat, east))
 
+    @pl.when(at_end)
+    def _():
+        greet((mid, lon))
+        greet((mid + 1, lon))
+
+    @pl.when(at_mid)
+    def _():
+        greet((0, lon))
+        greet((last, lon))
+
     loads = [
         pltpu.make_async_copy(x_hbm.at[:, :, rows], x.at[own], local.at[0]),
         pltpu.make_async_copy(t_hbm, t, local.at[1]),
@@ -192,8 +209,7 @@
     ]
     for copy in loads:
         copy.start()
-    ends = lat * (n_lat - 1 - lat)
-    pl.semaphore_wait(barrier, jnp.where(ends == 0, 3, 4))
+    pl.semaphore_wait(barrier, jnp.where(at_end, 5, jnp.where(at_mid, 6, 4)))
 
     def remote(src, dst, slot, where):
         return pltpu.make_async_remote_copy(
@@ -218,16 +234,50 @@
         remote(e.at[:, 1], e.at[:, 2], 7, (south, lon)),
     ]
 
+    first, second = passing.at[0], passing.at[1, pl.ds(0, 120)]
+    hop_up = [
+        remote(x_hbm.at[0, 1, pl.ds(0, 128)], first, 10, (0, lon)),
+        remote(x_hbm.at[0, 1, pl.ds(128, 120)], second, 11, (0, lon)),
+    ]
+    hop_down = [
+        remote(x_hbm.at[1, 1, pl.ds(128, 128)], first, 10, (last, lon)),
+        remote(x_hbm.at[1, 1, pl.ds(8, 120)], second, 11, (last, lon)),
+    ]
+    pass_up = [
+        remote(first, x.at[3, 1, pl.ds(0, 128)], 3, (mid, lon)),
+        remote(second, x.at[3, 1, pl.ds(128, 120)], 8, (mid, lon)),
+    ]
+    pass_down = [
+        remote(first, x.at[2, 1, pl.ds(128, 128)], 6, (mid + 1, lon)),
+        remote(second, x.at[2, 1, pl.ds(8, 120)], 9, (mid + 1, lon)),
+    ]
+
     def ends_do(act, which):
-        @pl.when(has_north)
+        for cond, copies, hops, turn in ((has_north, up, hop_up, mid + 1), (has_south, down, hop_down, mid)):
+            for i in which:
+                if i in (1, 2):
+                    @pl.when(cond & (lat != turn))
+                    def _():
+                        act(copies[i])
+
+                    @pl.when(lat == turn)
+                    def _():
+                        act(hops[i - 1])
+                else:
+                    @pl.when(cond)
+                    def _():
+                        act(copies[i])
+
+    def relay(i):
+        @pl.when(lat == 0)
         def _():
-            for i in which:
-                act(up[i])
-
-        @pl.when(has_south)
+            hop_up[i].wait_recv()
+            pass_up[i].start()
+
+        @pl.when(lat == last)
         def _():
-            for i in which:
-                act(down[i])
+            hop_down[i].wait_recv()
+            pass_down[i].start()
 
     def arrived(which):
         @pl.when(has_north)
@@ -296,7 +346,9 @@
     for copy in sides:
         copy.wait_recv()
     ends_do(lambda copy: copy.start(), (3, 2))
+    relay(0)
     centre(0, 1)
+    relay(1)
     for v in range(2):
         rims(0, v)
         along_lat(0, v)
@@ -310,6 +362,16 @@
     for copy in sides:
         copy.wait_send()
     ends_do(lambda copy: copy.wait_send(), (0, 1, 2, 3))
+
+    @pl.when(lat == 0)
+    def _():
+        for copy in pass_up:
+            copy.wait_send()
+
+    @pl.when(lat == last)
+    def _():
+        for copy in pass_down:
+            copy.wait_send()
 
 
 def filter_tile(n_lat, n_lon, x, weights):
@@ -324,8 +386,9 @@
             pltpu.VMEM((4, 2, 4, 256, 128), jnp.float32),
             pltpu.VMEM((2, 2, 768, 512), jnp.bfloat16),
             pltpu.VMEM((2, 2, 64, 192), jnp.bfloat16),
-            pltpu.SemaphoreType.DMA((10,)),
-            pltpu.SemaphoreType.DMA((10,)),
+            pltpu.VMEM((2, 128, 512), jnp.float32),
+            pltpu.SemaphoreType.DMA((12,)),
+            pltpu.SemaphoreType.DMA((12,)),
             pltpu.SemaphoreType.DMA((3,)),
         ],
         compiler_params=pltpu.CompilerParams(
@@ -337,8 +400,8 @@
 
 
 def route_kernel(n_lat, n_lon, obs_hbm, cells_hbm, counts_hbm, lengths_hbm, weights_hbm, mix_hbm,
-                 vals, cells, mixer, t_out, a_out,
-                 box, cell_box, counts, lengths, weights, mix, tiles, local, send, recv):
+                 vals, cells, mixer_hbm, t_hbm, a_hbm,
+                 box, cell_box, counts, lengths, weights, mix, tiles, mixer, t_out, a_out, local, send, recv):
     lat = lax.axis_index("lat")
     lon = lax.axis_index("lon")
     me = lat * n_lon + lon
@@ -448,6 +511,15 @@
     for i in range(8):
         mixer[pl.ds(i * 16, 16)] = jnp.where(col // 16 == i, small, 0.0)
 
+    writes = [
+        pltpu.make_async_copy(src, dst, local.at[i])
+        for i, (src, dst) in enumerate(((mixer, mixer_hbm), (t_out, t_hbm), (a_out, a_hbm)))
+    ]
+    for copy in writes:
+        copy.start()
+    for copy in writes:
+        copy.wait()
+
     rest = pl.ds(0, count - 1)
     for i, (src, dst) in enumerate(((box, vals), (cell_box, cells))):
         pltpu.make_async_copy(dst, dst, recv.at[i]).wait()
@@ -468,7 +540,7 @@
             jax.ShapeDtypeStruct((2, 2, 64, 192), bf16),
         ),
         in_specs=[hbm] * 6,
-        out_specs=[hbm] * 2 + [pl.BlockSpec(memory_space=pltpu.VMEM)] * 3,
+        out_specs=[hbm] * 5,
         scratch_shapes=[
             pltpu.VMEM((n, 16, 128), jnp.float32),
             pltpu.VMEM((n, 1, 128), jnp.int32),
@@ -477,6 +549,9 @@
             pltpu.SMEM((2, 3), jnp.float32),
             pltpu.SMEM((2, LEV, LEV), jnp.float32),
             pltpu.VMEM((2, 3, 128, 128), bf16),
+            pltpu.VMEM((128, 128), jnp.float32),
+            pltpu.VMEM((2, 2, 768, 512), bf16),
+            pltpu.VMEM((2, 2, 64, 192), bf16),
             pltpu.SemaphoreType.DMA((6,)),
             pltpu.SemaphoreType.DMA((2,)),
             pltpu.SemaphoreType.DMA((2,)),

time: 74 us -> 70.6 us (0.954)
  Pallas kernels: 72.5 us -> 68.6 us
    pallas_call x1, Pallas kernels: 24.1 us -> 22.4 us  [filter_tile(): pl.pallas_call(functools.partial(filter_kernel, n_lat, n_lon), out_shape=...]
    pallas_call x1, Pallas kernels: 25.2 us -> 23.5 us  [route(): pl.pallas_call(functools.partial(route_kernel, n_lat, n_lon), out_shape=(...]
where the time goes in v7:
time: 70.6 us; the launch traced here: 69.9 us
  Pallas kernels  68.6 us (97%)
  local copies, waits for them, and re-layouts  1.33 us (2%)
    pallas_call x1, Pallas kernels, route(): pl.pallas_call(functools.partial(route_kernel, n_lat, n_lon), out_shape=(...  23.5 us
    pallas_call x1, Pallas kernels, grid_tile(): pl.pallas_call(grid_kernel, out_shape=jax.ShapeDtypeStruct((2, 2, 36, 8,...  22.8 us
    pallas_call x1, Pallas kernels, filter_tile(): pl.pallas_call(functools.partial(filter_kernel, n_lat, n_lon), out_shape=...  22.4 us

profile of v7, /device:TPU:32, one launch (start us, length us, event | category | flops | bytes accessed | tf_op | source)
XLA Modules:
  0.0 69.9 jit_solution(2091922646917107679)
XLA Ops:
  0.0 23.5 %route.1 = (f32[128,16,128]{2,1,0:T(8,128)}, s32[128,1,128]{2,1,0:T(1,128)}, f32[128,128]{1,0:T(8,128)}, bf16[2,2,768,512]{3,2,1,0:T(8,128)(2,1)}, bf16[2,2,64,192]{3,2,1,0:T(8,128)(2,1)}) custom-call(f32[128,16,128]{2,1,0:T(8,128)} %bitcast.3, s32[128,1,128]{2,1,0:T(1,128)} %bitcast.4, s32[1,128]{1,0:T(1,128)} %counts_hbm.1, f32[2,3]{1,0:T(2,128)} %lengths_hbm.1, ...), custom_call_target="tpu_custom_call" | custom-call | flops 10000000 | bytes 4194304 | tf_op jit(solution)/shard_map/route/pallas_call | solution.py:533
  23.5 0.0 copy-start
  23.5 22.8 %scatter.1 = f32[2,2,36,8,512]{4,3,2,1,0:T(8,128)} custom-call(f32[128,16,128]{2,1,0:T(8,128)} %get-tuple-element.10.vals_hbm, s32[128,1,128]{2,1,0:T(1,128)} %get-tuple-element.11.cells_hbm, f32[128,128]{1,0:T(8,128)} %get-tuple-element.12.mixer_hbm), custom_call_target="tpu_custom_call" | custom-call | flops 1000000000 | bytes 4194304 | tf_op jit(solution)/shard_map/scatter/pallas_call | solution.py:139
  46.2 0.0 copy-done
  46.2 22.4 %filters.1 = f32[2,8,64,512]{3,2,1,0:T(8,128)S(1)} custom-call(f32[2,2,288,512]{3,2,1,0:T(8,128)} %bitcast.5, bf16[2,2,768,512]{3,2,1,0:T(8,128)(2,1)} %get-tuple-element.13.t_hbm, bf16[2,2,64,192]{3,2,1,0:T(8,128)(2,1)S(1)} %copy-done), custom_call_target="tpu_custom_call" | custom-call | flops 6000000000 | bytes 8388608 | tf_op jit(solution)/shard_map/filters/pallas_call | solution.py:378
  68.6 1.3 %copy.8 = f32[2,8,64,512]{3,2,1,0:T(8,128)} copy(f32[2,8,64,512]{3,2,1,0:T(8,128)S(1)} %filters.1) | data formatting | bytes 4194304
Async XLA Ops:
  23.5 22.8 %copy-start = (bf16[2,2,64,192]{3,2,1,0:T(8,128)(2,1)S(1)}, bf16[2,2,64,192]{3,2,1,0:T(8,128)(2,1)}, u32[]{:S(2)}) copy-start(bf16[2,2,64,192]{3,2,1,0:T(8,128)(2,1)} %get-tuple-element.14.a_hbm) | copy-start | bytes 294916

commit v8 on v7

--- a/solution.py
+++ b/solution.py
@@ -84,9 +84,10 @@
     lax.fori_loop(0, 128 // UNROLL, scatter, 0)
 
     r, c = lax.broadcasted_iota(jnp.int32, (128, 128), 0), lax.broadcasted_iota(jnp.int32, (128, 128), 1)
-    for rg in range(8):
-        hit = (lax.rem(r, 16) == lax.rem(c, 16)) & (r // 16 == rg)
-        picker[:, pl.ds(rg * 128, 128)] = jnp.where(hit, 1.0, 0.0).astype(jnp.bfloat16)
+    for q in range(4):
+        hit = (lax.rem(r, 16) == lax.rem(c, 16)) & (r // 16 == q + 4 * (c // 64))
+        picker[:, pl.ds(q * 128, 128)] = jnp.where(hit, 1.0, 0.0).astype(jnp.bfloat16)
+    low = lax.broadcasted_iota(jnp.int32, (512, 128), 1) < 64
 
     def write(k2):
         at = pl.ds(k2 * 4, 4)
@@ -96,10 +97,14 @@
         t = k2
         rows = 128 * BLOCKS
         base = t * rows
+        def total(rg):
+            at = pl.ds(pl.multiple_of(rg * 4096 + base, rows), rows)
+            return ga[at, :] + gb[at, :] + gc[at, :]
+
         parts = []
-        for rg in range(8):
-            at = pl.ds(pl.multiple_of(rg * 4096 + base, rows), rows)
-            parts.append(ga[at, :] + gb[at, :] + gc[at, :])
+        for q in range(4):
+            one, other = total(q), total(q + 4)
+            parts.append(jnp.where(low, one, other) + pltpu.roll(jnp.where(low, other, one), 64, 1))
         hi, lo = split(jnp.concatenate(parts, axis=1))
         dims = (((1,), (1,)), ((), ()))
         block = lax.dot_general(picker[...], hi, dims, preferred_element_type=jnp.float32)
@@ -146,7 +151,7 @@
             pltpu.VMEM((128, 128), jnp.float32),
             pltpu.VMEM((2048, 128), jnp.float32),
             pltpu.VMEM((2, 2, 36, 8, 512), jnp.float32),
-            pltpu.VMEM((128, 1024), jnp.bfloat16),
+            pltpu.VMEM((128, 512), jnp.bfloat16),
             pltpu.VMEM((128, 1, 128), jnp.int32),
             pltpu.SemaphoreType.DMA((4,)),
             pltpu.SemaphoreType.DMA((8,)),
@@ -426,8 +431,9 @@
             act(lat, columns[k])
 
         def line(i, carry):
+            away = jnp.where(i % 2 == 1, (i + 1) // 2, n_lat - i // 2)
             for column in columns:
-                act(lax.rem(lat + i, n_lat), column)
+                act(lax.rem(lat + away, n_lat), column)
             return carry
 
         lax.fori_loop(1, n_lat, line, 0)

time: 70.6 us -> 70.2 us (level)
    pallas_call x1, Pallas kernels: 23.5 us -> 24.5 us  [route(): pl.pallas_call(functools.partial(route_kernel, n_lat, n_lon), out_shape=(...]
    pallas_call x1, Pallas kernels: 22.4 us -> 21.5 us  [filter_tile(): pl.pallas_call(functools.partial(filter_kernel, n_lat, n_lon), out_shape=...]
where the time goes in v8:
time: 70.2 us; the launch traced here: 69.5 us
  Pallas kernels  68.1 us (97%)
  local copies, waits for them, and re-layouts  1.33 us (2%)
    pallas_call x1, Pallas kernels, route(): pl.pallas_call(functools.partial(route_kernel, n_lat, n_lon), out_shape=(...  24.5 us
    pallas_call x1, Pallas kernels, grid_tile(): pl.pallas_call(grid_kernel, out_shape=jax.ShapeDtypeStruct((2, 2, 36, 8,...  22.1 us
    pallas_call x1, Pallas kernels, filter_tile(): pl.pallas_call(functools.partial(filter_kernel, n_lat, n_lon), out_shape=...  21.5 us

profile of v8, /device:TPU:32, one launch (start us, length us, event | category | flops | bytes accessed | tf_op | source)
XLA Modules:
  0.0 69.5 jit_solution(1038393037692419183)
XLA Ops:
  0.0 24.5 %route.1 = (f32[128,16,128]{2,1,0:T(8,128)}, s32[128,1,128]{2,1,0:T(1,128)}, f32[128,128]{1,0:T(8,128)}, bf16[2,2,768,512]{3,2,1,0:T(8,128)(2,1)}, bf16[2,2,64,192]{3,2,1,0:T(8,128)(2,1)}) custom-call(f32[128,16,128]{2,1,0:T(8,128)} %bitcast.3, s32[128,1,128]{2,1,0:T(1,128)} %bitcast.4, s32[1,128]{1,0:T(1,128)} %counts_hbm.1, f32[2,3]{1,0:T(2,128)} %lengths_hbm.1, ...), custom_call_target="tpu_custom_call" | custom-call | flops 10000000 | bytes 4194304 | tf_op jit(solution)/shard_map/route/pallas_call | solution.py:539
  24.5 0.0 copy-start
  24.6 22.1 %scatter.1 = f32[2,2,36,8,512]{4,3,2,1,0:T(8,128)} custom-call(f32[128,16,128]{2,1,0:T(8,128)} %get-tuple-element.10.vals_hbm, s32[128,1,128]{2,1,0:T(1,128)} %get-tuple-element.11.cells_hbm, f32[128,128]{1,0:T(8,128)} %get-tuple-element.12.mixer_hbm), custom_call_target="tpu_custom_call" | custom-call | flops 1000000000 | bytes 4194304 | tf_op jit(solution)/shard_map/scatter/pallas_call | solution.py:144
  46.7 0.0 copy-done
  46.7 21.5 %filters.1 = f32[2,8,64,512]{3,2,1,0:T(8,128)S(1)} custom-call(f32[2,2,288,512]{3,2,1,0:T(8,128)} %bitcast.5, bf16[2,2,768,512]{3,2,1,0:T(8,128)(2,1)} %get-tuple-element.13.t_hbm, bf16[2,2,64,192]{3,2,1,0:T(8,128)(2,1)S(1)} %copy-done), custom_call_target="tpu_custom_call" | custom-call | flops 6000000000 | bytes 8388608 | tf_op jit(solution)/shard_map/filters/pallas_call | solution.py:383
  68.2 1.3 %copy.8 = f32[2,8,64,512]{3,2,1,0:T(8,128)} copy(f32[2,8,64,512]{3,2,1,0:T(8,128)S(1)} %filters.1) | data formatting | bytes 4194304
Async XLA Ops:
  24.5 22.1 %copy-start = (bf16[2,2,64,192]{3,2,1,0:T(8,128)(2,1)S(1)}, bf16[2,2,64,192]{3,2,1,0:T(8,128)(2,1)}, u32[]{:S(2)}) copy-start(bf16[2,2,64,192]{3,2,1,0:T(8,128)(2,1)} %get-tuple-element.14.a_hbm) | copy-start | bytes 294916

commit v9 on v8

--- a/solution.py
+++ b/solution.py
@@ -12,7 +12,6 @@
 NACC = 3
 UNROLL = 4
 AHEAD = 1
-BLOCKS = 4
 VMEM = 62 * 2**20
 MESH = pl.DeviceIdType.MESH
 
@@ -87,33 +86,32 @@
     for q in range(4):
         hit = (lax.rem(r, 16) == lax.rem(c, 16)) & (r // 16 == q + 4 * (c // 64))
         picker[:, pl.ds(q * 128, 128)] = jnp.where(hit, 1.0, 0.0).astype(jnp.bfloat16)
-    low = lax.broadcasted_iota(jnp.int32, (512, 128), 1) < 64
+    low = lax.broadcasted_iota(jnp.int32, (128, 128), 1) < 64
 
     def write(k2):
         at = pl.ds(k2 * 4, 4)
         return pltpu.make_async_copy(out.at[:, :, at], out_hbm.at[:, :, at], stores.at[k2])
 
     def gather(k2, carry):
-        t = k2
-        rows = 128 * BLOCKS
-        base = t * rows
-        def total(rg):
-            at = pl.ds(pl.multiple_of(rg * 4096 + base, rows), rows)
-            return ga[at, :] + gb[at, :] + gc[at, :]
-
-        parts = []
-        for q in range(4):
-            one, other = total(q), total(q + 4)
-            parts.append(jnp.where(low, one, other) + pltpu.roll(jnp.where(low, other, one), 64, 1))
-        hi, lo = split(jnp.concatenate(parts, axis=1))
-        dims = (((1,), (1,)), ((), ()))
-        block = lax.dot_general(picker[...], hi, dims, preferred_element_type=jnp.float32)
-        block = block + lax.dot_general(picker[...], lo, dims, preferred_element_type=jnp.float32)
-        block = block.reshape(8, 2, 8, rows)
-        at = pl.ds(pl.multiple_of(lax.rem(t, 4 // BLOCKS) * rows, rows), rows)
-        for v in range(2):
-            for h in range(2):
-                out[h, v, pl.ds(k2 * 4, 4), :, at] = block[h * 4 : h * 4 + 4, v]
+        for piece in range(4):
+            base = k2 * 512 + piece * 128
+
+            def total(rg):
+                at = pl.ds(pl.multiple_of(rg * 4096 + base, 128), 128)
+                return ga[at, :] + gb[at, :] + gc[at, :]
+
+            parts = []
+            for q in range(4):
+                one, other = total(q), total(q + 4)
+                parts.append(jnp.where(low, one, other) + pltpu.roll(jnp.where(low, other, one), 64, 1))
+            hi, lo = split(jnp.concatenate(parts, axis=1))
+            dims = (((1,), (1,)), ((), ()))
+            block = lax.dot_general(picker[...], hi, dims, preferred_element_type=jnp.float32)
+            block = block + lax.dot_general(picker[...], lo, dims, preferred_element_type=jnp.float32)
+            block = block.reshape(8, 2, 8, 128)
+            for v in range(2):
+                for h in range(2):
+                    out[h, v, pl.ds(k2 * 4, 4), :, pl.ds(piece * 128, 128)] = block[h * 4 : h * 4 + 4, v]
         write(k2).start()
         return carry
 

time: 70.2 us -> 69.6 us (level)
  no operation moved by 1% of the time
where the time goes in v9:
time: 69.6 us; the launch traced here: 68.9 us
  Pallas kernels  67.5 us (97%)
  local copies, waits for them, and re-layouts  1.33 us (2%)
    pallas_call x1, Pallas kernels, route(): pl.pallas_call(functools.partial(route_kernel, n_lat, n_lon), out_shape=(...  24.5 us
    pallas_call x1, Pallas kernels, filter_tile(): pl.pallas_call(functools.partial(filter_kernel, n_lat, n_lon), out_shape=...  21.5 us
    pallas_call x1, Pallas kernels, grid_tile(): pl.pallas_call(grid_kernel, out_shape=jax.ShapeDtypeStruct((2, 2, 36, 8,...  21.5 us

profile of v9, /device:TPU:32, one launch (start us, length us, event | category | flops | bytes accessed | tf_op | source)
XLA Modules:
  0.0 68.9 jit_solution(10701418915900672037)
XLA Ops:
  0.0 24.5 %route.1 = (f32[128,16,128]{2,1,0:T(8,128)}, s32[128,1,128]{2,1,0:T(1,128)}, f32[128,128]{1,0:T(8,128)}, bf16[2,2,768,512]{3,2,1,0:T(8,128)(2,1)}, bf16[2,2,64,192]{3,2,1,0:T(8,128)(2,1)}) custom-call(f32[128,16,128]{2,1,0:T(8,128)} %bitcast.3, s32[128,1,128]{2,1,0:T(1,128)} %bitcast.4, s32[1,128]{1,0:T(1,128)} %counts_hbm.1, f32[2,3]{1,0:T(2,128)} %lengths_hbm.1, ...), custom_call_target="tpu_custom_call" | custom-call | flops 10000000 | bytes 4194304 | tf_op jit(solution)/shard_map/route/pallas_call | solution.py:537
  24.5 0.0 copy-start
  24.6 21.5 %scatter.1 = f32[2,2,36,8,512]{4,3,2,1,0:T(8,128)} custom-call(f32[128,16,128]{2,1,0:T(8,128)} %get-tuple-element.10.vals_hbm, s32[128,1,128]{2,1,0:T(1,128)} %get-tuple-element.11.cells_hbm, f32[128,128]{1,0:T(8,128)} %get-tuple-element.12.mixer_hbm), custom_call_target="tpu_custom_call" | custom-call | flops 1000000000 | bytes 4194304 | tf_op jit(solution)/shard_map/scatter/pallas_call | solution.py:142
  46.0 0.0 copy-done
  46.0 21.5 %filters.1 = f32[2,8,64,512]{3,2,1,0:T(8,128)S(1)} custom-call(f32[2,2,288,512]{3,2,1,0:T(8,128)} %bitcast.5, bf16[2,2,768,512]{3,2,1,0:T(8,128)(2,1)} %get-tuple-element.13.t_hbm, bf16[2,2,64,192]{3,2,1,0:T(8,128)(2,1)S(1)} %copy-done), custom_call_target="tpu_custom_call" | custom-call | flops 6000000000 | bytes 8388608 | tf_op jit(solution)/shard_map/filters/pallas_call | solution.py:381
  67.6 1.3 %copy.8 = f32[2,8,64,512]{3,2,1,0:T(8,128)} copy(f32[2,8,64,512]{3,2,1,0:T(8,128)S(1)} %filters.1) | data formatting | bytes 4194304
Async XLA Ops:
  24.5 21.5 %copy-start = (bf16[2,2,64,192]{3,2,1,0:T(8,128)(2,1)S(1)}, bf16[2,2,64,192]{3,2,1,0:T(8,128)(2,1)}, u32[]{:S(2)}) copy-start(bf16[2,2,64,192]{3,2,1,0:T(8,128)(2,1)} %get-tuple-element.14.a_hbm) | copy-start | bytes 294916
